TPU v7x, 32 devices: a whole 2x2x4 slice. The times are simulated.
32 devices in a mesh: lon: 8 (over z, core), lat: 4 (over y, x).
Axes of the slice: x: 2, y: 2, z: 4, core: 2. Of those that a mesh axis runs over, the one named last changes fastest.
Arguments:
- zonal_current: float32 [32, 256, 1024], P(None, 'lat', 'lon'), may hold values from -6 to 6
- meridional_current: float32 [32, 256, 1024], P(None, 'lat', 'lon'), may hold values from -6 to 6
- warmth_anomaly: float32 [32, 256, 1024], P(None, 'lat', 'lon'), may hold values from -6 to 6
- brine_anomaly: float32 [32, 256, 1024], P(None, 'lat', 'lon'), may hold values from -6 to 6
- marine_indicator: int32 [256, 1024], P('lat', 'lon'), may hold values 0 or 1
- retained_tile_indicator: int32 [16, 64], P('lat', 'lon'), may hold values 0 or 1
- seabed_thickness: float32 [256, 1024], P('lat', 'lon'), may hold values from 0.25 to 2.5
- elevation_pivot_entry: float32 [256, 1024], P('lat', 'lon'), may hold values from 0.1 to 1
Outputs:
- zonal_next: float32 [32, 256, 1024], P(None, 'lat', 'lon')
- meridional_next: float32 [32, 256, 1024], P(None, 'lat', 'lon')
- temperature_next: float32 [32, 256, 1024], P(None, 'lat', 'lon')
- salinity_next: float32 [32, 256, 1024], P(None, 'lat', 'lon')
- surface_pressure: float32 [256, 1024], P('lat', 'lon')
- pressure_residual: float32 [256, 1024], P('lat', 'lon')
All inputs are finite; a program needn't handle non-finite values. No bound on the sum of `marine_indicator` or of `retained_tile_indicator` on one device may be relied on, other than what follows from the above.
Results may differ from a plain program's by a relative error of at most 0.0003.
Values sent between devices are 32-bit elements; how exact they have to be, the bound alone decides.
A program may use at most 128 MiB of HBM per device.

v0:
```python
import jax
import jax.numpy as jnp
from jax import lax
from jax.sharding import PartitionSpec as P

BLK = 16
ITERS = 3


time_step = 0.1
viscosity = 0.2
diffusivity = 0.15
thermal = 0.2
haline = 0.8
source_gain = 8.0


def extended(cells, sides, width):
    for axis, dim in sides:
        count = lax.axis_size(axis)
        head = lax.slice_in_dim(cells, 0, width, axis=dim)
        tail = lax.slice_in_dim(cells, cells.shape[dim] - width, cells.shape[dim], axis=dim)
        cells = jnp.concatenate(
            [
                lax.ppermute(tail, axis, [(i, (i + 1) % count) for i in range(count)]),
                cells,
                lax.ppermute(head, axis, [((i + 1) % count, i) for i in range(count)]),
            ],
            axis=dim,
        )
    return cells


def partner(block, axis, stride):
    count = lax.axis_size(axis)
    route = []
    for low in range(count):
        high = low | 1 << stride
        if high != low and high < count:
            route += [(low, high), (high, low)]
    return lax.ppermute(block, axis, route)


def neighbours(fields, parity):
    padded = extended(fields, (("lon", 2), ("lat", 1)), 1)
    top_row = fields[:, fields.shape[1] - 1, :]
    bit_count = lax.axis_size("lon").bit_length() - 1
    bit_order = list(range(bit_count))
    mirror = top_row
    for bit_number in bit_order:
        mirror = partner(mirror, "lon", bit_number)
    mirror = mirror[:, ::-1]
    lat_index = lax.axis_index("lat")
    north_row = jnp.where(
        lat_index == lax.axis_size("lat") - 1, parity[:, None] * mirror, padded[:, -1, 1:-1]
    )
    south_row = jnp.where(lat_index == 0, jnp.zeros_like(top_row), padded[:, 0, 1:-1])
    east_cell = padded[:, 1:-1, 2:]
    west_cell = padded[:, 1:-1, :-2]
    north_cell = jnp.concatenate([padded[:, 2:-1, 1:-1], north_row[:, None, :]], axis=1)
    south_cell = jnp.concatenate([south_row[:, None, :], padded[:, 1:-2, 1:-1]], axis=1)
    return (east_cell, west_cell, north_cell, south_cell)


def laplace(field, near):
    return near[0] + near[1] + near[2] + near[3] - 4.0 * field


def pick(near, first, count):
    return tuple((item[first : first + count] for item in near))


def precond_sum(residual, precond):
    return lax.psum(jnp.sum(residual * precond), ("lon", "lat"))


def local(
    zonal_current,
    meridional_current,
    warmth_anomaly,
    brine_anomaly,
    marine_indicator,
    retained_tile_indicator,
    seabed_thickness,
    elevation_pivot_entry,
):
    level_fields, height, breadth = zonal_current.shape
    marine_snapshot = marine_indicator.astype(jnp.float32)
    zonal = zonal_current * marine_snapshot
    merid = meridional_current * marine_snapshot
    enthalpy_content = warmth_anomaly * marine_snapshot
    salt = brine_anomaly * marine_snapshot
    fields = jnp.concatenate([zonal, merid, enthalpy_content, salt], axis=0)
    parity = jnp.concatenate(
        [-jnp.ones((2 * level_fields,), jnp.float32), jnp.ones((2 * level_fields,), jnp.float32)]
    )
    near_all = neighbours(fields, parity)
    near_u = pick(near_all, 0, level_fields)
    near_v = pick(near_all, level_fields, level_fields)
    near_t = pick(near_all, 2 * level_fields, level_fields)
    near_s = pick(near_all, 3 * level_fields, level_fields)
    near_p = tuple(
        (jnp.cumsum(haline * near_s[side] - thermal * near_t[side], axis=0) for side in range(4))
    )
    total_rows = height * lax.axis_size("lat")
    rows_global = (lax.axis_index("lat") * height + jnp.arange(height)).astype(jnp.float32)
    coriolis = (2.0 * (rows_global + 0.5) / total_rows - 1.0)[:, None]
    zonal_next = marine_snapshot * (
        zonal
        + time_step
        * (coriolis * merid - 0.5 * (near_p[0] - near_p[1]) + viscosity * laplace(zonal, near_u))
    )
    merid_next = marine_snapshot * (
        merid
        + time_step
        * (-coriolis * zonal - 0.5 * (near_p[2] - near_p[3]) + viscosity * laplace(merid, near_v))
    )
    tracers = []
    for tracer, near_q in ((enthalpy_content, near_t), (salt, near_s)):
        flux = 0.5 * (
            near_u[0] * near_q[0]
            - near_u[1] * near_q[1]
            + near_v[2] * near_q[2]
            - near_v[3] * near_q[3]
        )
        tracers.append(
            marine_snapshot * (tracer + time_step * (-flux + diffusivity * laplace(tracer, near_q)))
        )
    zonal_mean = jnp.sum(zonal_next, axis=0) / level_fields
    merid_mean = jnp.sum(merid_next, axis=0) / level_fields
    kept = jnp.repeat(
        jnp.repeat(retained_tile_indicator.astype(jnp.float32), BLK, axis=0), BLK, axis=1
    )
    open_cells = marine_snapshot * kept
    column = seabed_thickness * open_cells
    surface = jnp.stack([zonal_mean, merid_mean, column], axis=0)
    near_b = neighbours(surface, jnp.array([-1.0, -1.0, 1.0], jnp.float32))
    rhs = (
        -source_gain
        * open_cells
        * 0.5
        * (near_b[0][0] - near_b[1][0] + near_b[2][1] - near_b[3][1])
    )
    weights = [0.5 * (column + near_b[side][2]) for side in range(4)]
    diag = elevation_pivot_entry + weights[0] + weights[1] + weights[2] + weights[3]
    unit_parity = jnp.ones((1,), jnp.float32)
    solution = jnp.zeros_like(rhs)
    residual = rhs
    precond = residual / diag
    direction = precond
    product_now = precond_sum(residual, precond)
    for step in range(ITERS):
        near_x = neighbours(direction[None], unit_parity)
        image = open_cells * (
            diag * direction
            - weights[0] * near_x[0][0]
            - weights[1] * near_x[1][0]
            - weights[2] * near_x[2][0]
            - weights[3] * near_x[3][0]
        )
        alpha = product_now / lax.psum(jnp.sum(direction * image), ("lon", "lat"))
        solution = solution + alpha * direction
        residual = residual - alpha * image
        if step + 1 < ITERS:
            precond = residual / diag
            product_next = precond_sum(residual, precond)
            direction = precond + product_next / product_now * direction
            product_now = product_next
    return (zonal_next, merid_next, tracers[0], tracers[1], solution, residual)


def solution(mesh):
    in_specs = (
        P(None, "lat", "lon"),
        P(None, "lat", "lon"),
        P(None, "lat", "lon"),
        P(None, "lat", "lon"),
        P("lat", "lon"),
        P("lat", "lon"),
        P("lat", "lon"),
        P("lat", "lon"),
    )
    out_specs = (
        P(None, "lat", "lon"),
        P(None, "lat", "lon"),
        P(None, "lat", "lon"),
        P(None, "lat", "lon"),
        P("lat", "lon"),
        P("lat", "lon"),
    )
    return jax.shard_map(local, mesh=mesh, in_specs=in_specs, out_specs=out_specs, check_vma=False)
```

profile of v0, /device:TPU:0, one launch (start us, length us, event | category | flops | bytes accessed | tf_op | source)
XLA Modules:
  0.0 366.2 jit_solution(1731860227714545735)
XLA Ops:
  1.4 2.8 broadcast_multiply_fusion.3
  5.7 4.7 %fusion.127 = (f32[128,64,1]{2,1,0:T(8,128)}, f32[128,64,1]{2,1,0:T(8,128)}) fusion(f32[128,64,128]{2,1,0:T(8,128)S(1)} %pad_maximum_fusion), kind=kLoop, calls=%fused_computation.225 | loop fusion | bytes 131072 | tf_op jit(solution)/shard_map/slice | solution.py:22
  10.3 3.7 %copy.93 = f32[128,64,1]{0,1,2:T(8,128)S(1)} copy(f32[128,64,1]{2,1,0:T(8,128)} %get-tuple-element.72) | data formatting | bytes 65536 | tf_op jit(solution)/shard_map/slice | solution.py:22
  14.6 3.7 %copy.91 = f32[128,64,1]{0,1,2:T(8,128)S(1)} copy(f32[128,64,1]{2,1,0:T(8,128)} %get-tuple-element.73) | data formatting | bytes 65536 | tf_op jit(solution)/shard_map/slice | solution.py:21
  18.3 4.1 %collective-permute-start = (f32[128,64,1]{0,1,2:T(8,128)S(1)}, f32[128,64,1]{0,1,2:T(8,128)S(1)}, u32[]{:S(2)}, u32[]{:S(2)}) collective-permute-start(f32[128,64,1]{0,1,2:T(8,128)S(1)} %copy.91), channel_id=1, source_target_pairs={{4,0},{8,4},{12,8},{16,12},{20,16},{24,20},{28,24},{0,28},{5,1},{9... | collective-permute-start | bytes 98312 | tf_op jit(solution)/shard_map/ppermute | solution.py:27
  22.4 4.6 %copy.95 = f32[128,64,128]{2,0,1:T(8,128)S(1)} copy(f32[128,64,128]{2,1,0:T(8,128)} %copy-done) | data formatting | bytes 8388608 | tf_op jit(solution)/shard_map/concatenate | solution.py:93
  27.0 2.0 copy-done.9
  29.7 4.4 %fusion.126 = (f32[128,63,128]{2,1,0:T(8,128)}, f32[128,63,128]{2,1,0:T(8,128)}) fusion(f32[128,64,128]{2,1,0:T(8,128)S(1)} %copy-done.1), kind=kLoop, calls=%fused_computation.224 | loop fusion | bytes 16515072 | tf_op jit(solution)/shard_map/slice | solution.py:60
  34.5 2.7 copy.96
  37.2 2.6 copy.98
  39.8 1.8 pad_maximum_fusion.19
  41.6 2.0 collective-permute-start.6
  44.5 4.4 %copy.94 = f32[128,64,1]{2,1,0:T(8,128)} copy(f32[128,64,1]{0,1,2:T(8,128)S(1)} %collective-permute-done.1) | data formatting | bytes 65536 | tf_op jit(solution)/shard_map/ppermute | solution.py:25
  49.0 2.1 pad_maximum_fusion.14
  52.5 1.1 fusion.31
  53.6 4.4 %copy.92 = f32[128,64,1]{2,1,0:T(8,128)} copy(f32[128,64,1]{0,1,2:T(8,128)S(1)} %collective-permute-done) | data formatting | bytes 65536 | tf_op jit(solution)/shard_map/ppermute | solution.py:27
  58.0 4.2 %pad_maximum_fusion.16 = (f32[32,64,128]{2,1,0:T(8,128)}, f32[32,64,128]{2,1,0:T(8,128)}) fusion(f32[128,64,1]{2,1,0:T(8,128)} %copy.92, f32[32,64,128]{2,1,0:T(8,128)S(1)} %get-tuple-element.100, f32[32,64,128]{2,1,0:T(8,128)S(1)} %get-tuple-element.99, f32[32,64,128]{2,1,0:T(8,128)} %copy-done.7, f32[32,64,128]{2,1,0:T(8,128)S(1)} %get-tuple-element.98), kind=kLoop, calls=%fused_computation.51 | loop fusion | flops 2097152 | bytes 6324224 | tf_op jit(solution)/shard_map/slice | solution.py:70
  63.6 3.1 collective-permute-done.3
  66.7 1.4 collective-permute-start.4
  68.1 1.3 fusion.23
  69.4 3.1 collective-permute-done.4
  74.5 7.9 %fusion.123 = (f32[64,128]{1,0:T(8,128)S(1)}, f32[32,64,128]{2,1,0:T(8,128)}, f32[32,64,128]{2,1,0:T(8,128)}, f32[32,64,128]{2,1,0:T(8,128)}) fusion(f32[32,64,128]{2,1,0:T(8,128)} %copy-done.7, f32[32,64,128]{2,1,0:T(8,128)S(1)} %get-tuple-element.100, f32[32,64,128]{2,1,0:T(8,128)S(1)} %get-tuple-element.99, f32[32,64,128]{2,1,0:T(8,128)S(1)} %get-tuple-element.98, ...), kind=kOutput, calls=%fused_computation.222 | output fusion | flops 15982592 | bytes 29622784 | tf_op jit(solution)/shard_map/jit(cumsum)/reduce_window_sum | solution.py:103
  82.4 1.4 copy-done.5
  83.9 1.2 copy-done.6
  86.2 6.3 %fusion.121 = (f32[64,128]{1,0:T(8,128)S(1)}, f32[32,64,128]{2,1,0:T(8,128)}, f32[32,64,128]{2,1,0:T(8,128)}, f32[32,64,128]{2,1,0:T(8,128)}) fusion(f32[128,63,128]{2,1,0:T(8,128)S(1)} %copy-done.4, f32[128,1,128]{2,1,0:T(1,128)S(1)} %bitcast.213, f32[128,1,128]{2,1,0:T(1,128)S(1)} %bitcast.209, f32[128,63,128]{2,1,0:T(8,128)S(1)} %copy-done.2, ...), kind=kOutput, calls=%fused_computation.221 | output fusion | flops 15982592 | bytes 21102848 | tf_op jit(solution)/shard_map/jit(cumsum)/reduce_window_sum | solution.py:103
  92.7 2.6 collective-permute-start.7
  95.3 4.9 %add_multiply_fusion = (f32[32,64,128]{2,1,0:T(8,128)}, f32[32,64,128]{2,1,0:T(8,128)}) fusion(f32[32,64,128]{2,1,0:T(8,128)S(1)} %copy-done.14, f32[32,64,128]{2,1,0:T(8,128)S(1)} %copy-done.11, f32[32,64,128]{2,1,0:T(8,128)} %get-tuple-element.59, f32[32,64,128]{2,1,0:T(8,128)} %get-tuple-element.58, f32[32,64,128]{2,1,0:T(8,128)} %get-tuple-element.54, ...), kind=kLoop, calls=%fused_computation.52 | loop fusion | flops 11534336 | bytes 21004288 | tf_op jit(solution)/shard_map/mul | solution.py:127
  101.9 2.4 collective-permute-start.12
  104.3 1.2 collective-permute-done.10
  106.0 4.0 %collective-permute-done.11 = f32[3,128]{1,0:T(4,128)S(1)} collective-permute-done((f32[3,128]{1,0:T(4,128)S(1)}, f32[3,128]{1,0:T(4,128)S(1)}, u32[]{:S(2)}, u32[]{:S(2)}) %collective-permute-start.11) | collective-permute-done | bytes 1568 | tf_op jit(solution)/shard_map/ppermute | solution.py:41
  112.0 3.5 collective-permute-done.15
  115.7 2.4 collective-permute-start.20
  118.7 2.9 collective-permute-done.17
  121.7 4.4 %collective-permute-done.18 = f32[1,128]{1,0:T(1,128)S(1)} collective-permute-done((f32[1,128]{1,0:T(1,128)S(1)}, f32[1,128]{1,0:T(1,128)S(1)}, u32[]{:S(2)}, u32[]{:S(2)}) %collective-permute-start.18) | collective-permute-done | bytes 544 | tf_op jit(solution)/shard_map/ppermute | solution.py:41
  126.9 38.2 %all-reduce = (f32[]{:T(128)}, f32[]{:T(128)}) all-reduce(f32[]{:T(128)} %get-tuple-element.31, f32[]{:T(128)} %get-tuple-element.30), channel_id=1, replica_groups=mesh['lon'=8,'lat'=4] {'lon','lat'}, use_global_device_ids=true, to_apply=%region_7.8 | all-reduce | flops 2 | bytes 16 | tf_op jit(solution)/shard_map/psum | solution.py:74
  167.0 41.0 %psum.44 = f32[]{:T(128)} all-reduce(f32[]{:T(128)} %get-tuple-element.41), channel_id=1, replica_groups=mesh['lon'=8,'lat'=4] {'lon','lat'}, use_global_device_ids=true, to_apply=%region_11.12 | all-reduce | flops 1 | bytes 8 | tf_op jit(solution)/shard_map/psum | solution.py:74
  210.4 1.1 collective-permute-done.21
  211.5 3.5 collective-permute-done.22
  215.0 2.2 collective-permute-start.27
  218.2 2.6 collective-permute-done.24
  220.9 4.4 %collective-permute-done.25 = f32[1,128]{1,0:T(1,128)S(1)} collective-permute-done((f32[1,128]{1,0:T(1,128)S(1)}, f32[1,128]{1,0:T(1,128)S(1)}, u32[]{:S(2)}, u32[]{:S(2)}) %collective-permute-start.25) | collective-permute-done | bytes 544 | tf_op jit(solution)/shard_map/ppermute | solution.py:41
  226.1 37.9 %psum.45 = f32[]{:T(128)} all-reduce(f32[]{:T(128)} %get-tuple-element.39), channel_id=1, replica_groups=mesh['lon'=8,'lat'=4] {'lon','lat'}, use_global_device_ids=true, to_apply=%region_13.14 | all-reduce | flops 1 | bytes 8 | tf_op jit(solution)/shard_map/psum | solution.py:161
  266.0 41.8 %psum.46 = f32[]{:T(128)} all-reduce(f32[]{:T(128)} %get-tuple-element.36), channel_id=1, replica_groups=mesh['lon'=8,'lat'=4] {'lon','lat'}, use_global_device_ids=true, to_apply=%region_15.16 | all-reduce | flops 1 | bytes 8 | tf_op jit(solution)/shard_map/psum | solution.py:74
  311.3 3.5 collective-permute-done.29
  314.8 2.0 collective-permute-start.34
  317.8 2.5 collective-permute-done.31
  320.4 4.4 %collective-permute-done.32 = f32[1,128]{1,0:T(1,128)S(1)} collective-permute-done((f32[1,128]{1,0:T(1,128)S(1)}, f32[1,128]{1,0:T(1,128)S(1)}, u32[]{:S(2)}, u32[]{:S(2)}) %collective-permute-start.32) | collective-permute-done | bytes 544 | tf_op jit(solution)/shard_map/ppermute | solution.py:41
  325.6 37.9 %psum.47 = f32[]{:T(128)} all-reduce(f32[]{:T(128)} %get-tuple-element.34), channel_id=1, replica_groups=mesh['lon'=8,'lat'=4] {'lon','lat'}, use_global_device_ids=true, to_apply=%region_17.18 | all-reduce | flops 1 | bytes 8 | tf_op jit(solution)/shard_map/psum | solution.py:161
  (149 shorter events, 26.2 us)
Async XLA Ops:
  14.1 20.5 %collective-permute-start.1 = (f32[128,64,1]{0,1,2:T(8,128)S(1)}, f32[128,64,1]{0,1,2:T(8,128)S(1)}, u32[]{:S(2)}, u32[]{:S(2)}) collective-permute-start(f32[128,64,1]{0,1,2:T(8,128)S(1)} %copy.93), channel_id=1, source_target_pairs={{0,4},{4,8},{8,12},{12,16},{16,20},{20,24},{24,28},{28,0},{1,5},{5... | collective-permute-start | bytes 98312 | tf_op jit(solution)/shard_map/ppermute | solution.py:25
  18.3 11.4 %copy-start.1 = (f32[128,64,128]{2,1,0:T(8,128)S(1)}, f32[128,64,128]{2,1,0:T(8,128)}, u32[]{:S(2)}) copy-start(f32[128,64,128]{2,1,0:T(8,128)} %copy-done) | copy-start | bytes 12582916
  18.3 18.9 %collective-permute-start = (f32[128,64,1]{0,1,2:T(8,128)S(1)}, f32[128,64,1]{0,1,2:T(8,128)S(1)}, u32[]{:S(2)}, u32[]{:S(2)}) collective-permute-start(f32[128,64,1]{0,1,2:T(8,128)S(1)} %copy.91), channel_id=1, source_target_pairs={{4,0},{8,4},{12,8},{16,12},{20,16},{24,20},{28,24},{0,28},{5,1},{9... | collective-permute-start | bytes 98312 | tf_op jit(solution)/shard_map/ppermute | solution.py:27
  29.7 32.6 %collective-permute-start.2 = (f32[128,128]{1,0:T(8,128)}, f32[128,128]{1,0:T(8,128)}, u32[]{:S(2)}, u32[]{:S(2)}) collective-permute-start(f32[128,128]{1,0:T(8,128)} %slice_bitcast_fusion.1), channel_id=1, source_target_pairs={{0,4},{4,0},{8,12},{12,8},{16,20},{20,16},{24,28},{28,24},{1,5},{5... | collective-permute-start | bytes 196616 | tf_op jit(solution)/shard_map/ppermute | solution.py:41
  41.6 21.0 %collective-permute-start.6 = (f32[128,1,130]{2,0,1:T(8,128)}, f32[128,1,130]{2,0,1:T(8,128)}, u32[]{:S(2)}, u32[]{:S(2)}) collective-permute-start(f32[128,1,130]{2,0,1:T(8,128)} %get-tuple-element.65), channel_id=1, source_target_pairs={{0,1},{1,2},{2,3},{3,0},{4,5},{5,6},{6,7},{7,4},{8,9},{9,10},{10,1... | collective-permute-start | bytes 199688 | tf_op jit(solution)/shard_map/ppermute | solution.py:25
  43.6 29.8 %collective-permute-start.5 = (f32[128,1,130]{2,0,1:T(8,128)S(1)}, f32[128,1,130]{2,0,1:T(8,128)}, u32[]{:S(2)}, u32[]{:S(2)}) collective-permute-start(f32[128,1,130]{2,0,1:T(8,128)S(1)} %get-tuple-element.64), channel_id=1, source_target_pairs={{1,0},{2,1},{3,2},{0,3},{5,4},{6,5},{7,6},{4,7},{9,8},{10,9},{11,1... | collective-permute-start | bytes 199688 | tf_op jit(solution)/shard_map/ppermute | solution.py:27
  58.0 10.0 %copy-start.3 = (f32[128,63,128]{2,1,0:T(8,128)S(1)}, f32[128,63,128]{2,1,0:T(8,128)}, u32[]{:S(2)}) copy-start(f32[128,63,128]{2,1,0:T(8,128)} %get-tuple-element.71) | copy-start | bytes 12386308
  62.2 11.2 %copy-start.21 = (f32[128]{0:T(128)S(1)}, f32[128]{0:T(128)}, u32[]{:S(2)}) copy-start(f32[128]{0:T(128)} %constant.15.clone.1) | copy-start | bytes 1540
  62.2 4.5 %collective-permute-start.3 = (f32[128,128]{1,0:T(8,128)}, f32[128,128]{1,0:T(8,128)S(1)}, u32[]{:S(2)}, u32[]{:S(2)}) collective-permute-start(f32[128,128]{1,0:T(8,128)} %collective-permute-done.2), channel_id=1, source_target_pairs={{0,8},{8,0},{4,12},{12,4},{16,24},{24,16},{20,28},{28,20},{1,9},{9... | collective-permute-start | bytes 196616 | tf_op jit(solution)/shard_map/ppermute | solution.py:41
  66.7 5.8 %collective-permute-start.4 = (f32[128,128]{1,0:T(8,128)S(1)}, f32[128,128]{1,0:T(8,128)}, u32[]{:S(2)}, u32[]{:S(2)}) collective-permute-start(f32[128,128]{1,0:T(8,128)S(1)} %collective-permute-done.3), channel_id=1, source_target_pairs={{0,16},{16,0},{4,20},{20,4},{8,24},{24,8},{12,28},{28,12},{1,17},{... | collective-permute-start | bytes 196616 | tf_op jit(solution)/shard_map/ppermute | solution.py:41
  74.4 9.4 %copy-start.5 = (f32[128,64,1]{2,1,0:T(8,128)S(1)}, f32[128,64,1]{2,1,0:T(8,128)}, u32[]{:S(2)}) copy-start(f32[128,64,1]{2,1,0:T(8,128)} %copy.94) | copy-start | bytes 98308
  74.5 10.6 %copy-start.6 = (f32[128,64,1]{2,1,0:T(8,128)S(1)}, f32[128,64,1]{2,1,0:T(8,128)}, u32[]{:S(2)}) copy-start(f32[128,64,1]{2,1,0:T(8,128)} %copy.92) | copy-start | bytes 98308
  74.5 10.8 %copy-start.8 = (f32[32,64,128]{2,1,0:T(8,128)S(1)}, f32[32,64,128]{2,1,0:T(8,128)}, u32[]{:S(2)}) copy-start(f32[32,64,128]{2,1,0:T(8,128)} %copy-done.7) | copy-start | bytes 3145732
  74.5 11.1 %copy-start.14 = (f32[32,64,128]{2,1,0:T(8,128)S(1)}, f32[32,64,128]{2,1,0:T(8,128)}, u32[]{:S(2)}) copy-start(f32[32,64,128]{2,1,0:T(8,128)} %get-tuple-element.68) | copy-start | bytes 3145732
  74.5 11.4 %copy-start.15 = (f32[32,64,128]{2,1,0:T(8,128)S(1)}, f32[32,64,128]{2,1,0:T(8,128)}, u32[]{:S(2)}) copy-start(f32[32,64,128]{2,1,0:T(8,128)} %get-tuple-element.69) | copy-start | bytes 3145732
  74.5 11.7 %copy-start.16 = (f32[32,64,128]{2,1,0:T(8,128)S(1)}, f32[32,64,128]{2,1,0:T(8,128)}, u32[]{:S(2)}) copy-start(f32[32,64,128]{2,1,0:T(8,128)} %fusion.31) | copy-start | bytes 3145732
  86.2 9.1 %copy-start.11 = (f32[32,64,128]{2,1,0:T(8,128)S(1)}, f32[32,64,128]{2,1,0:T(8,128)}, u32[]{:S(2)}) copy-start(f32[32,64,128]{2,1,0:T(8,128)} %copy-done.10) | copy-start | bytes 3145732
  86.2 9.1 %copy-start.13 = (f32[32,64,128]{2,1,0:T(8,128)S(1)}, f32[32,64,128]{2,1,0:T(8,128)}, u32[]{:S(2)}) copy-start(f32[32,64,128]{2,1,0:T(8,128)} %copy-done.12) | copy-start | bytes 3145732
  92.5 9.4 %collective-permute-start.9 = (f32[3,128]{1,0:T(4,128)S(1)}, f32[3,128]{1,0:T(4,128)S(1)}, u32[]{:S(2)}, u32[]{:S(2)}) collective-permute-start(f32[3,128]{1,0:T(4,128)S(1)} %bitcast.220), channel_id=1, source_target_pairs={{0,4},{4,0},{8,12},{12,8},{16,20},{20,16},{24,28},{28,24},{1,5},{5... | collective-permute-start | bytes 4616 | tf_op jit(solution)/shard_map/ppermute | solution.py:41
  92.7 7.6 %collective-permute-start.7 = (f32[3,64,1]{2,1,0:T(8,128)S(1)}, f32[3,64,1]{2,1,0:T(8,128)S(1)}, u32[]{:S(2)}, u32[]{:S(2)}) collective-permute-start(f32[3,64,1]{2,1,0:T(8,128)S(1)} %get-tuple-element.85), channel_id=1, source_target_pairs={{4,0},{8,4},{12,8},{16,12},{20,16},{24,20},{28,24},{0,28},{5,1},{9... | collective-permute-start | bytes 2312 | tf_op jit(solution)/shard_map/ppermute | solution.py:27
  95.3 5.8 %collective-permute-start.8 = (f32[3,64,1]{2,1,0:T(8,128)S(1)}, f32[3,64,1]{2,1,0:T(8,128)S(1)}, u32[]{:S(2)}, u32[]{:S(2)}) collective-permute-start(f32[3,64,1]{2,1,0:T(8,128)S(1)} %get-tuple-element.84), channel_id=1, source_target_pairs={{0,4},{4,8},{8,12},{12,16},{16,20},{20,24},{24,28},{28,0},{1,5},{5... | collective-permute-start | bytes 2312 | tf_op jit(solution)/shard_map/ppermute | solution.py:25
  95.3 14.7 %copy-start.22 = (f32[3]{0:T(128)S(1)}, f32[3]{0:T(128)}, u32[]{:S(2)}) copy-start(f32[3]{0:T(128)} %constant.55.clone) | copy-start | bytes 40
  95.3 14.8 %copy-start.19 = (f32[64,128]{1,0:T(8,128)S(1)}, f32[64,128]{1,0:T(8,128)}, u32[]{:S(2)}) copy-start(f32[64,128]{1,0:T(8,128)} %param.16) | copy-start | bytes 98308
  101.2 4.5 %collective-permute-start.13 = (f32[3,1,130]{2,1,0:T(1,128)S(1)}, f32[3,1,130]{2,1,0:T(1,128)S(1)}, u32[]{:S(2)}, u32[]{:S(2)}) collective-permute-start(f32[3,1,130]{2,1,0:T(1,128)S(1)} %get-tuple-element.74), channel_id=1, source_target_pairs={{0,1},{1,2},{2,3},{3,0},{4,5},{5,6},{6,7},{7,4},{8,9},{9,10},{10,1... | collective-permute-start | bytes 4688 | tf_op jit(solution)/shard_map/ppermute | solution.py:25
  101.9 3.6 collective-permute-start.10
  101.9 4.0 %collective-permute-start.12 = (f32[3,1,130]{2,1,0:T(1,128)S(1)}, f32[3,1,130]{2,1,0:T(1,128)S(1)}, u32[]{:S(2)}, u32[]{:S(2)}) collective-permute-start(f32[3,1,130]{2,1,0:T(1,128)S(1)} %get-tuple-element.75), channel_id=1, source_target_pairs={{1,0},{2,1},{3,2},{0,3},{5,4},{6,5},{7,6},{4,7},{9,8},{10,9},{11,1... | collective-permute-start | bytes 4688 | tf_op jit(solution)/shard_map/ppermute | solution.py:27
  105.5 4.5 %collective-permute-start.11 = (f32[3,128]{1,0:T(4,128)S(1)}, f32[3,128]{1,0:T(4,128)S(1)}, u32[]{:S(2)}, u32[]{:S(2)}) collective-permute-start(f32[3,128]{1,0:T(4,128)S(1)} %collective-permute-done.10), channel_id=1, source_target_pairs={{0,16},{16,0},{4,20},{20,4},{8,24},{24,8},{12,28},{28,12},{1,17},{... | collective-permute-start | bytes 4616 | tf_op jit(solution)/shard_map/ppermute | solution.py:41
  110.3 1.7 collective-permute-start.14
  110.4 5.1 %collective-permute-start.15 = (f32[1,64,1]{2,1,0:T(8,128)S(1)}, f32[1,64,1]{2,1,0:T(8,128)S(1)}, u32[]{:S(2)}, u32[]{:S(2)}) collective-permute-start(f32[1,64,1]{2,1,0:T(8,128)S(1)} %get-tuple-element.96), channel_id=1, source_target_pairs={{0,4},{4,8},{8,12},{12,16},{16,20},{20,24},{24,28},{28,0},{1,5},{5... | collective-permute-start | bytes 776 | tf_op jit(solution)/shard_map/ppermute | solution.py:25
  110.9 7.2 %collective-permute-start.16 = (f32[1,128]{1,0:T(1,128)S(1)}, f32[1,128]{1,0:T(1,128)S(1)}, u32[]{:S(2)}, u32[]{:S(2)}) collective-permute-start(f32[1,128]{1,0:T(1,128)S(1)} %slice_bitcast_fusion.7), channel_id=1, source_target_pairs={{0,4},{4,0},{8,12},{12,8},{16,20},{20,16},{24,28},{28,24},{1,5},{5... | collective-permute-start | bytes 1544 | tf_op jit(solution)/shard_map/ppermute | solution.py:41
  115.7 5.9 %collective-permute-start.20 = (f32[1,1,130]{2,1,0:T(1,128)S(1)}, f32[1,1,130]{2,1,0:T(1,128)S(1)}, u32[]{:S(2)}, u32[]{:S(2)}) collective-permute-start(f32[1,1,130]{2,1,0:T(1,128)S(1)} %get-tuple-element.81), channel_id=1, source_target_pairs={{0,1},{1,2},{2,3},{3,0},{4,5},{5,6},{6,7},{7,4},{8,9},{9,10},{10,1... | collective-permute-start | bytes 1568 | tf_op jit(solution)/shard_map/ppermute | solution.py:25
  118.1 3.5 collective-permute-start.17
  118.1 8.1 %collective-permute-start.19 = (f32[1,1,130]{2,1,0:T(1,128)S(1)}, f32[1,1,130]{2,1,0:T(1,128)S(1)}, u32[]{:S(2)}, u32[]{:S(2)}) collective-permute-start(f32[1,1,130]{2,1,0:T(1,128)S(1)} %get-tuple-element.80), channel_id=1, source_target_pairs={{1,0},{2,1},{3,2},{0,3},{5,4},{6,5},{7,6},{4,7},{9,8},{10,9},{11,1... | collective-permute-start | bytes 1568 | tf_op jit(solution)/shard_map/ppermute | solution.py:27
  121.6 4.4 %collective-permute-start.18 = (f32[1,128]{1,0:T(1,128)S(1)}, f32[1,128]{1,0:T(1,128)S(1)}, u32[]{:S(2)}, u32[]{:S(2)}) collective-permute-start(f32[1,128]{1,0:T(1,128)S(1)} %collective-permute-done.17), channel_id=1, source_target_pairs={{0,16},{16,0},{4,20},{20,4},{8,24},{24,8},{12,28},{28,12},{1,17},{... | collective-permute-start | bytes 1544 | tf_op jit(solution)/shard_map/ppermute | solution.py:41
  209.4 2.1 collective-permute-start.21
  209.8 5.1 %collective-permute-start.22 = (f32[1,64,1]{2,1,0:T(8,128)S(1)}, f32[1,64,1]{2,1,0:T(8,128)S(1)}, u32[]{:S(2)}, u32[]{:S(2)}) collective-permute-start(f32[1,64,1]{2,1,0:T(8,128)S(1)} %get-tuple-element.92), channel_id=1, source_target_pairs={{0,4},{4,8},{8,12},{12,16},{16,20},{20,24},{24,28},{28,0},{1,5},{5... | collective-permute-start | bytes 776 | tf_op jit(solution)/shard_map/ppermute | solution.py:25
  209.9 7.3 %collective-permute-start.23 = (f32[1,128]{1,0:T(1,128)S(1)}, f32[1,128]{1,0:T(1,128)S(1)}, u32[]{:S(2)}, u32[]{:S(2)}) collective-permute-start(f32[1,128]{1,0:T(1,128)S(1)} %slice_bitcast_fusion.5), channel_id=1, source_target_pairs={{0,4},{4,0},{8,12},{12,8},{16,20},{20,16},{24,28},{28,24},{1,5},{5... | collective-permute-start | bytes 1544 | tf_op jit(solution)/shard_map/ppermute | solution.py:41
  215.0 5.8 %collective-permute-start.27 = (f32[1,1,130]{2,1,0:T(1,128)S(1)}, f32[1,1,130]{2,1,0:T(1,128)S(1)}, u32[]{:S(2)}, u32[]{:S(2)}) collective-permute-start(f32[1,1,130]{2,1,0:T(1,128)S(1)} %get-tuple-element.79), channel_id=1, source_target_pairs={{0,1},{1,2},{2,3},{3,0},{4,5},{5,6},{6,7},{7,4},{8,9},{9,10},{10,1... | collective-permute-start | bytes 1568 | tf_op jit(solution)/shard_map/ppermute | solution.py:25
  217.3 3.5 collective-permute-start.24
  217.3 8.1 %collective-permute-start.26 = (f32[1,1,130]{2,1,0:T(1,128)S(1)}, f32[1,1,130]{2,1,0:T(1,128)S(1)}, u32[]{:S(2)}, u32[]{:S(2)}) collective-permute-start(f32[1,1,130]{2,1,0:T(1,128)S(1)} %get-tuple-element.78), channel_id=1, source_target_pairs={{1,0},{2,1},{3,2},{0,3},{5,4},{6,5},{7,6},{4,7},{9,8},{10,9},{11,1... | collective-permute-start | bytes 1568 | tf_op jit(solution)/shard_map/ppermute | solution.py:27
  220.8 4.4 %collective-permute-start.25 = (f32[1,128]{1,0:T(1,128)S(1)}, f32[1,128]{1,0:T(1,128)S(1)}, u32[]{:S(2)}, u32[]{:S(2)}) collective-permute-start(f32[1,128]{1,0:T(1,128)S(1)} %collective-permute-done.24), channel_id=1, source_target_pairs={{0,16},{16,0},{4,20},{20,4},{8,24},{24,8},{12,28},{28,12},{1,17},{... | collective-permute-start | bytes 1544 | tf_op jit(solution)/shard_map/ppermute | solution.py:41
  309.2 2.1 collective-permute-start.28
  309.6 5.1 %collective-permute-start.29 = (f32[1,64,1]{2,1,0:T(8,128)S(1)}, f32[1,64,1]{2,1,0:T(8,128)S(1)}, u32[]{:S(2)}, u32[]{:S(2)}) collective-permute-start(f32[1,64,1]{2,1,0:T(8,128)S(1)} %get-tuple-element.88), channel_id=1, source_target_pairs={{0,4},{4,8},{8,12},{12,16},{16,20},{20,24},{24,28},{28,0},{1,5},{5... | collective-permute-start | bytes 776 | tf_op jit(solution)/shard_map/ppermute | solution.py:25
  309.8 7.0 %collective-permute-start.30 = (f32[1,128]{1,0:T(1,128)S(1)}, f32[1,128]{1,0:T(1,128)S(1)}, u32[]{:S(2)}, u32[]{:S(2)}) collective-permute-start(f32[1,128]{1,0:T(1,128)S(1)} %slice_bitcast_fusion.3), channel_id=1, source_target_pairs={{0,4},{4,0},{8,12},{12,8},{16,20},{20,16},{24,28},{28,24},{1,5},{5... | collective-permute-start | bytes 1544 | tf_op jit(solution)/shard_map/ppermute | solution.py:41
  314.8 5.5 %collective-permute-start.34 = (f32[1,1,130]{2,1,0:T(1,128)S(1)}, f32[1,1,130]{2,1,0:T(1,128)S(1)}, u32[]{:S(2)}, u32[]{:S(2)}) collective-permute-start(f32[1,1,130]{2,1,0:T(1,128)S(1)} %get-tuple-element.77), channel_id=1, source_target_pairs={{0,1},{1,2},{2,3},{3,0},{4,5},{5,6},{6,7},{7,4},{8,9},{9,10},{10,1... | collective-permute-start | bytes 1568 | tf_op jit(solution)/shard_map/ppermute | solution.py:25
  316.8 3.5 collective-permute-start.31
  316.8 8.1 %collective-permute-start.33 = (f32[1,1,130]{2,1,0:T(1,128)S(1)}, f32[1,1,130]{2,1,0:T(1,128)S(1)}, u32[]{:S(2)}, u32[]{:S(2)}) collective-permute-start(f32[1,1,130]{2,1,0:T(1,128)S(1)} %get-tuple-element.76), channel_id=1, source_target_pairs={{1,0},{2,1},{3,2},{0,3},{5,4},{6,5},{7,6},{4,7},{9,8},{10,9},{11,1... | collective-permute-start | bytes 1568 | tf_op jit(solution)/shard_map/ppermute | solution.py:27
  320.3 4.4 %collective-permute-start.32 = (f32[1,128]{1,0:T(1,128)S(1)}, f32[1,128]{1,0:T(1,128)S(1)}, u32[]{:S(2)}, u32[]{:S(2)}) collective-permute-start(f32[1,128]{1,0:T(1,128)S(1)} %collective-permute-done.31), channel_id=1, source_target_pairs={{0,16},{16,0},{4,20},{20,4},{8,24},{24,8},{12,28},{28,12},{1,17},{... | collective-permute-start | bytes 1544 | tf_op jit(solution)/shard_map/ppermute | solution.py:41
  (10 other events, 40.0 us)
where the time goes:
time: 367 us; the launch traced here: 366 us
  blocking collectives  197 us (54%)
  waiting for transfers between devices  47.1 us (13%)
  local copies, waits for them, and re-layouts  46.1 us (13%)
  other arithmetic  41.4 us (11%)
  starting transfers between devices  27.1 us (7%)
  between operations  7.74 us (2%)
    psum x3, blocking collectives, precond_sum(): return lax.psum(jnp.sum(residual * precond), ('lon', 'lat'))  121 us
    psum x2, blocking collectives, local(): alpha = product_now / lax.psum(jnp.sum(direction * image), ('lon', 'lat'))  75.8 us
    ppermute x15, waiting for transfers between devices, partner(): return lax.ppermute(block, axis, route)  32.5 us
    another operation x4, other arithmetic, local(): jnp.cumsum(haline * near_s[side] - thermal * near_t[side], axis=0)  16.6 us
    ppermute x10, starting transfers between devices, extended(): lax.ppermute(head, axis, [((i + 1) % count, i) for i in range(count)])  13.5 us
    ppermute x10, waiting for transfers between devices, extended(): lax.ppermute(tail, axis, [(i, (i + 1) % count) for i in range(count)])  11.6 us
    ppermute x10, starting transfers between devices, extended(): lax.ppermute(tail, axis, [(i, (i + 1) % count) for i in range(count)])  10.4 us
    slice x6, local copies, waits for them, and re-layouts, extended(): lax.slice_in_dim(cells, cells.shape[dim] - width, cells.shape[dim], axis=...  8.71 us
  transfers between devices with their start and end apart: 35, of which 19 were waited for; matrix products, arithmetic and copies ran while one was open for 13% of the time, Pallas kernels for 0%

commit v1 on v0

v1 whole, which is shorter than its diff:
```python
import functools

import jax
import jax.numpy as jnp
from jax import lax
from jax.experimental import pallas as pl
from jax.experimental.pallas import tpu as pltpu
from jax.sharding import PartitionSpec as P

BLK = 16
ITERS = 3

time_step = 0.1
viscosity = 0.2
diffusivity = 0.15
thermal = 0.2
haline = 0.8
source_gain = 8.0

NF = 4
NA = 6
STRIP = 16
S8 = 8
QROWS = 16
PAD = 8


def reverse_lanes(x):
    index = x.shape[-1] - 1 - lax.broadcasted_iota(jnp.int32, x.shape, x.ndim - 1)
    return jnp.take_along_axis(x, index, axis=x.ndim - 1, mode="promise_in_bounds")


def roll(x, shift, axis):
    return pltpu.roll(x, shift % x.shape[axis], axis)


def near(x):
    return roll(x, -1, 1), roll(x, 1, 1), roll(x, -1, 0), roll(x, 1, 0)


def surface_kernel(
    u_ref, v_ref, t_ref, s_ref, marine_ref, kept_ref, depth_ref, elev_ref,
    edge_ref, rows_ref, sol_ref, res_ref,
    held, send_e, send_w, send_v, recv_e, recv_w, recv_v, recv_c, ext,
    part_lon, part_lat, load_sem, send_sem, recv_sem, lon_send, lon_recv, lat_send, lat_recv,
):
    n_lon, n_lat = lax.axis_size("lon"), lax.axis_size("lat")
    lon, lat = lax.axis_index("lon"), lax.axis_index("lat")
    levels, height, breadth = u_ref.shape
    last = lat == n_lat - 1
    east, west = lax.rem(lon + 1, n_lon), lax.rem(lon + n_lon - 1, n_lon)
    mirror = n_lon - 1 - lon

    fields = (u_ref, v_ref, t_ref, s_ref)
    quarters = height // QROWS
    loads = []
    for q in range(quarters):
        row = []
        for f in range(NF):
            copy = pltpu.make_async_copy(
                fields[f].at[:, pl.ds(q * QROWS, QROWS), :],
                held.at[f, :, pl.ds(q * QROWS, QROWS), :],
                load_sem.at[q, f],
            )
            copy.start()
            row.append(copy)
        loads.append(row)

    barrier = pltpu.get_barrier_semaphore()

    def greet(a, b):
        pl.semaphore_signal(
            barrier, inc=1, device_id={"lon": a, "lat": b}, device_id_type=pl.DeviceIdType.MESH
        )

    for o in range(1, n_lon):
        greet(lax.rem(lon + o, n_lon), lat)
    for o in range(1, n_lat):
        greet(lon, lax.rem(lat + o, n_lat))

    @pl.when(lat > 0)
    def _():
        greet(east, lat - 1)
        greet(west, lat - 1)

    @pl.when(lat < n_lat - 1)
    def _():
        greet(east, lat + 1)
        greet(west, lat + 1)

    lane = lax.broadcasted_iota(jnp.int32, (height, breadth), 1)
    ocean = marine_ref[...].astype(jnp.float32)
    bands = []
    lane_band = lax.broadcasted_iota(jnp.int32, (BLK, breadth), 1) // BLK
    for jb in range(height // BLK):
        band = jnp.zeros((BLK, breadth), jnp.float32)
        for ib in range(breadth // BLK):
            band = jnp.where(lane_band == ib, kept_ref[jb, ib].astype(jnp.float32), band)
        bands.append(band)
    kept = jnp.concatenate(bands, axis=0)
    ext[0, PAD : PAD + height, 0:breadth] = ocean
    ext[1, PAD : PAD + height, 0:breadth] = depth_ref[...] * (ocean * kept)
    ext[2, PAD : PAD + height, 0:breadth] = elev_ref[...]

    lane_q = lax.broadcasted_iota(jnp.int32, (QROWS, breadth), 1)
    even_q = lax.rem(lane_q, 2) == 0
    for q in range(quarters):
        for copy in loads[q]:
            copy.wait()
        r0 = q * QROWS

        def level_step(l, carry, r0=r0, q=q):
            even, odd, su, sv, sp = carry
            weight = (levels - l).astype(jnp.float32) * (1.0 / levels)
            x = [held[f, l, r0 : r0 + QROWS, :] for f in range(NF)]
            for f in range(NF):
                k = NF * l + f
                turned = pltpu.roll(x[f], k, 1)
                before = jnp.where(k == 0, breadth - 1, k - 1)
                here = (lane_q == k) | (lane_q == before)
                if f % 2 == 0:
                    even = jnp.where(here, turned, even)
                else:
                    odd = jnp.where(here, turned, odd)
                if q == 0:
                    send_v[0, pl.ds(f * levels + l, 1), :] = held[f, l, 0:1, :]
                if q == quarters - 1:
                    send_v[1, pl.ds(f * levels + l, 1), :] = held[f, l, height - 1 : height, :]
            su = su + x[0]
            sv = sv + x[1]
            sp = sp + weight * (haline * x[3] - thermal * x[2])
            return even, odd, su, sv, sp

        zero = jnp.zeros((QROWS, breadth), jnp.float32)
        even, odd, su, sv, sp = lax.fori_loop(0, levels, level_step, (zero,) * 5, unroll=2)
        mask = ext[0, PAD + r0 : PAD + r0 + QROWS, 0:breadth]
        head = jnp.where(even_q, even, odd) * mask[:, 0:1]
        tail = jnp.where(even_q, odd, even) * mask[:, breadth - 1 : breadth]
        send_w[0, r0 : r0 + QROWS, :] = head
        send_e[0, r0 : r0 + QROWS, :] = tail
        inv = 1.0 / levels
        ext[3, PAD + r0 : PAD + r0 + QROWS, 0:breadth] = su * inv * mask
        ext[4, PAD + r0 : PAD + r0 + QROWS, 0:breadth] = sv * inv * mask
        ext[5, PAD + r0 : PAD + r0 + QROWS, 0:breadth] = sp * mask

    packed = jnp.zeros((height, breadth), jnp.float32)
    for a in range(NA):
        x = ext[a, PAD : PAD + height, 0:breadth]
        packed = jnp.where(lane // STRIP == a, roll(x, STRIP * a + S8, 1), packed)
        n3 = NF * levels + S8 * a
        send_v[0, n3 : n3 + S8, :] = x[0:S8, :]
        send_v[1, n3 : n3 + S8, :] = x[height - S8 : height, :]
    send_e[1] = packed
    send_w[1] = packed
    for f in range(NF):
        send_v[0, f * levels : (f + 1) * levels, :] *= ocean[0:1, :]
        send_v[1, f * levels : (f + 1) * levels, :] *= ocean[height - 1 : height, :]

    count = (
        (n_lon - 1) + (n_lat - 1)
        + 2 * (lat > 0).astype(jnp.int32) + 2 * (lat < n_lat - 1).astype(jnp.int32)
    )
    pl.semaphore_wait(barrier, count)

    def remote(src, dst, number, recv_number, a, b):
        return pltpu.make_async_remote_copy(
            src_ref=src, dst_ref=dst,
            send_sem=send_sem.at[number], recv_sem=recv_sem.at[recv_number],
            device_id={"lon": a, "lat": b}, device_id_type=pl.DeviceIdType.MESH,
        )

    up_slot = jnp.where(last, 1, 0)
    up_lat = jnp.where(last, lat, lat + 1)
    up_lon = jnp.where(last, mirror, lon)
    up_e = jnp.where(last, lax.rem(mirror + 1, n_lon), west)
    up_w = jnp.where(last, lax.rem(mirror + n_lon - 1, n_lon), east)
    top = send_e.at[1, pl.ds(height - S8, S8), :]
    bottom = send_e.at[1, pl.ds(0, S8), :]
    go_up = remote(send_v.at[1], recv_v.at[up_slot], 2, 2 + up_slot, up_lon, up_lat)
    go_e = remote(send_e, recv_w, 0, 0, east, lat)
    go_w = remote(send_w, recv_e, 1, 1, west, lat)
    go_up_e = remote(top, recv_c.at[up_slot, 0], 4, 4 + 2 * up_slot, up_e, up_lat)
    go_up_w = remote(top, recv_c.at[up_slot, 1], 5, 5 + 2 * up_slot, up_w, up_lat)
    down_lat = jnp.where(lat > 0, lat - 1, lat + 1)
    go_down = remote(send_v.at[0], recv_v.at[1], 3, 3, lon, down_lat)
    go_down_e = remote(bottom, recv_c.at[1, 0], 6, 6, west, down_lat)
    go_down_w = remote(bottom, recv_c.at[1, 1], 7, 7, east, down_lat)
    self_e = last & (up_e == lon)
    self_w = last & (up_w == lon)
    go_up.start()
    go_e.start()
    go_w.start()

    @pl.when(lat > 0)
    def _():
        go_down.start()
        go_down_e.start()
        go_down_w.start()

    @pl.when(jnp.logical_not(self_e))
    def _():
        go_up_e.start()

    @pl.when(jnp.logical_not(self_w))
    def _():
        go_up_w.start()

    @pl.when(self_e)
    def _():
        recv_c[1, 0] = send_e[1, height - S8 : height, :]

    @pl.when(self_w)
    def _():
        recv_c[1, 1] = send_e[1, height - S8 : height, :]

    def arrive(dst, recv_number):
        remote(dst, dst, 0, recv_number, east, lat).wait_recv()

    arrive(recv_w, 0)
    arrive(recv_e, 1)
    arrive(recv_v.at[1], 3)

    @pl.when(jnp.logical_not(self_e))
    def _():
        arrive(recv_c.at[1, 0], 6)

    @pl.when(jnp.logical_not(self_w))
    def _():
        arrive(recv_c.at[1, 1], 7)

    @pl.when(lat > 0)
    def _():
        arrive(recv_v.at[0], 2)
        arrive(recv_c.at[0, 0], 4)
        arrive(recv_c.at[0, 1], 5)

    @pl.when(lat == 0)
    def _():
        recv_v[0] = jnp.zeros(recv_v.shape[1:], jnp.float32)
        recv_c[0] = jnp.zeros(recv_c.shape[1:], jnp.float32)

    even_lane = lax.rem(lane, 2) == 0
    edge_ref[0] = jnp.where(even_lane, recv_e[0], recv_w[0])
    edge_ref[1] = jnp.where(even_lane, recv_w[0], recv_e[0])
    for f in range(NF):
        rows_ref[0, f] = recv_v[0, f * levels : (f + 1) * levels, :]
        top_rows = recv_v[1, f * levels : (f + 1) * levels, :]
        turned = reverse_lanes(top_rows)
        rows_ref[1, f] = jnp.where(last, -turned if f < 2 else turned, top_rows)

    strip_e = lax.rem(lane, STRIP) >= S8
    halo_lane = (lane < S8) | (lane >= breadth - S8)
    side = jnp.where(strip_e, recv_e[1], recv_w[1])
    c_lane = lax.broadcasted_iota(jnp.int32, (S8, breadth), 1)
    c_strip_e = lax.rem(c_lane, STRIP) >= S8
    c_halo = (c_lane < S8) | (c_lane >= breadth - S8)
    corner = [jnp.where(c_strip_e, recv_c[j, 0], recv_c[j, 1]) for j in range(2)]
    end = PAD + height
    for a in range(NA):
        fill = 1.0 if a == 2 else 0.0
        shift = -(STRIP * a + S8)
        ext[a, PAD:end, breadth : 2 * breadth] = jnp.where(halo_lane, roll(side, shift, 1), fill)
        n3 = NF * levels + S8 * a
        s_mid = recv_v[0, n3 : n3 + S8, :]
        s_out = jnp.where(c_halo, roll(corner[0], shift, 1), fill)
        if a == 2:
            s_mid = jnp.where(lat == 0, 1.0, s_mid)
            s_out = jnp.where(lat == 0, 1.0, s_out)
        ext[a, 0:PAD, 0:breadth] = s_mid
        ext[a, 0:PAD, breadth : 2 * breadth] = s_out
        sign = -1.0 if a in (3, 4) else 1.0
        n_mid = recv_v[1, n3 : n3 + S8, :]
        n_out = jnp.where(c_halo, roll(corner[1], shift, 1), fill)
        for at, block in ((0, n_mid), (breadth, n_out)):
            turned = sign * reverse_lanes(block)
            turned = jnp.concatenate([turned[i : i + 1] for i in range(S8 - 1, -1, -1)], axis=0)
            ext[a, end : end + PAD, at : at + breadth] = jnp.where(last, turned, block)

    rows = lax.broadcasted_iota(jnp.int32, (height + 2 * PAD, 2 * breadth), 0) + (lat * height - PAD)
    total_rows = n_lat * height
    rows = jnp.where(rows >= total_rows, 2 * total_rows - 1 - rows, rows)
    coriolis = 2.0 * (rows.astype(jnp.float32) + 0.5) / total_rows - 1.0
    ocean_x, column, um, vm, pm = ext[0], ext[1], ext[3], ext[4], ext[5]
    nu, nv, np_ = near(um), near(vm), near(pm)
    u_mean = ocean_x * (
        um + time_step * (
            coriolis * vm - 0.5 * (np_[0] - np_[1])
            + viscosity * (nu[0] + nu[1] + nu[2] + nu[3] - 4.0 * um)
        )
    )
    v_mean = ocean_x * (
        vm + time_step * (
            -coriolis * um - 0.5 * (np_[2] - np_[3])
            + viscosity * (nv[0] + nv[1] + nv[2] + nv[3] - 4.0 * vm)
        )
    )
    is_open = column > 0.0
    nc = near(column)
    weights = [0.5 * (column + c) for c in nc]
    diag = ext[2] + weights[0] + weights[1] + weights[2] + weights[3]
    scale = jnp.where(is_open, 1.0 / diag, 0.0)
    rhs = (-0.5 * source_gain) * (
        roll(u_mean, -1, 1) - roll(u_mean, 1, 1) + roll(v_mean, -1, 0) - roll(v_mean, 1, 0)
    )
    basis = [scale * rhs]
    for _ in range(ITERS):
        ny = near(basis[-1])
        total = weights[0] * ny[0] + weights[1] * ny[1] + weights[2] * ny[2] + weights[3] * ny[3]
        basis.append(scale * total)
    inner = [y[PAD:end, 0:breadth] for y in basis]
    weight_in = diag[PAD:end, 0:breadth]
    weighted = [weight_in * y for y in inner]
    moments = []
    for m in range(2 * ITERS):
        moments.append(jnp.sum(inner[m // 2] * weighted[(m + 1) // 2], axis=0, keepdims=True))
    while len(moments) < 8:
        moments.append(jnp.zeros((1, breadth), jnp.float32))
    tile = jnp.concatenate(moments, axis=0)

    def gather_sum(tile, parts, me, n, sends, recvs, axis):
        parts[me] = tile
        copies = []
        for o in range(1, n):
            to = lax.rem(me + o, n)
            copy = pltpu.make_async_remote_copy(
                src_ref=parts.at[me], dst_ref=parts.at[me],
                send_sem=sends.at[o - 1], recv_sem=recvs.at[o - 1],
                device_id={axis: to}, device_id_type=pl.DeviceIdType.MESH,
            )
            copy.start()
            copies.append(copy)
        for o in range(1, n):
            source = lax.rem(me + n - o, n)
            pltpu.make_async_remote_copy(
                src_ref=parts.at[source], dst_ref=parts.at[source],
                send_sem=sends.at[o - 1], recv_sem=recvs.at[o - 1],
                device_id={axis: source}, device_id_type=pl.DeviceIdType.MESH,
            ).wait_recv()
        total = parts[0]
        for i in range(1, n):
            total = total + parts[i]
        return total, copies

    tile, lon_copies = gather_sum(tile, part_lon, lon, n_lon, lon_send, lon_recv, "lon")
    tile, lat_copies = gather_sum(tile, part_lat, lat, n_lat, lat_send, lat_recv, "lat")
    sums = jnp.broadcast_to(jnp.sum(tile, axis=1, keepdims=True), tile.shape)
    m = [sums[i : i + 1, :] for i in range(2 * ITERS)]

    def dot(a, b):
        total = 0.0
        for i, p in enumerate(a):
            for j, q in enumerate(b):
                total = total + (p * q) * m[i + j]
        return total

    one = jnp.ones((1, breadth), jnp.float32)
    z, d = [one], [one]
    x = []
    rz = m[0]
    for step in range(ITERS):
        image = [d[0]] + [d[i] - d[i - 1] for i in range(1, len(d))] + [-d[-1]]
        alpha = rz / dot(d, image)
        x = [alpha * d[i] + (x[i] if i < len(x) else 0.0) for i in range(len(d))]
        z = [(z[i] if i < len(z) else 0.0) - alpha * image[i] for i in range(len(image))]
        if step + 1 < ITERS:
            rz_new = dot(z, z)
            beta = rz_new / rz
            d = [z[i] + (beta * d[i] if i < len(d) else 0.0) for i in range(len(z))]
            rz = rz_new
    answer = x[0] * inner[0]
    for i in range(1, ITERS):
        answer = answer + x[i] * inner[i]
    left = z[0] * weighted[0]
    for i in range(1, ITERS + 1):
        left = left + z[i] * weighted[i]
    sol_ref[...] = answer
    res_ref[...] = left

    go_up.wait_send()
    go_e.wait_send()
    go_w.wait_send()

    @pl.when(lat > 0)
    def _():
        go_down.wait_send()
        go_down_e.wait_send()
        go_down_w.wait_send()

    @pl.when(jnp.logical_not(self_e))
    def _():
        go_up_e.wait_send()

    @pl.when(jnp.logical_not(self_w))
    def _():
        go_up_w.wait_send()

    for copy in lon_copies + lat_copies:
        copy.wait_send()


def update_kernel(
    u_ref, v_ref, t_ref, s_ref, marine_ref, edge_ref, rows_ref,
    u_out, v_out, t_out, s_out,
    held, done, padded, slope, load_sem, store_sem,
):
    lat = lax.axis_index("lat")
    levels, height, breadth = u_ref.shape
    fields, outs = (u_ref, v_ref, t_ref, s_ref), (u_out, v_out, t_out, s_out)
    chunk = 4 if levels % 4 == 0 else 1
    chunks = levels // chunk

    def load(c, f):
        part = pl.ds(c * chunk, chunk)
        return pltpu.make_async_copy(fields[f].at[part], held.at[f, part], load_sem.at[c, f])

    def store(c, f):
        part = pl.ds(c * chunk, chunk)
        return pltpu.make_async_copy(done.at[f, part], outs[f].at[part], store_sem.at[c, f])

    for c in range(chunks):
        for f in range(NF):
            load(c, f).start()
    slope[...] = jnp.zeros_like(slope)
    total_rows = lax.axis_size("lat") * height
    lane = lax.broadcasted_iota(jnp.int32, (8, breadth), 1)
    first_lane, last_lane = lane == 0, lane == breadth - 1
    row8 = lax.broadcasted_iota(jnp.int32, (8, breadth), 0)
    mul_q = (time_step * viscosity, time_step * viscosity, time_step * diffusivity, time_step * diffusivity)

    def level_step(l, carry):
        b = lax.rem(l, 2)
        for f in range(NF):
            padded[b, f, PAD - 1 : PAD, :] = rows_ref[0, f, pl.ds(l, 1), :]
            padded[b, f, PAD + height : PAD + height + 1, :] = rows_ref[1, f, pl.ds(l, 1), :]
            for g in range(height // 8):
                mask = marine_ref[8 * g : 8 * g + 8, :].astype(jnp.float32)
                padded[b, f, PAD + 8 * g : PAD + 8 * g + 8, :] = held[f, l, 8 * g : 8 * g + 8, :] * mask
        for g in range(height // 8):
            r = 8 * g
            mask = marine_ref[r : r + 8, :].astype(jnp.float32)
            coriolis = (
                2.0 * ((row8 + (lat * height + r)).astype(jnp.float32) + 0.5) / total_rows - 1.0
            ) * time_step
            x, e, w, n, s = [], [], [], [], []
            for f in range(NF):
                at = PAD + r
                here = padded[b, f, at : at + 8, :]
                k = NF * l + f
                halo = pltpu.roll(
                    edge_ref[f % 2, r : r + 8, :], jnp.where(k == 0, 0, breadth - k), 1
                )
                x.append(here)
                e.append(pltpu.roll(jnp.where(first_lane, halo, here), breadth - 1, 1))
                w.append(pltpu.roll(jnp.where(last_lane, halo, here), 1, 1))
                n.append(padded[b, f, at + 1 : at + 9, :])
                s.append(padded[b, f, at - 1 : at + 7, :])
            gx = slope[0, r : r + 8, :] + (haline * (e[3] - w[3]) - thermal * (e[2] - w[2]))
            gy = slope[1, r : r + 8, :] + (haline * (n[3] - s[3]) - thermal * (n[2] - s[2]))
            slope[0, r : r + 8, :] = gx
            slope[1, r : r + 8, :] = gy
            new = [
                x[f] + mul_q[f] * (e[f] + w[f] + n[f] + s[f] - 4.0 * x[f]) for f in range(NF)
            ]
            new[0] = new[0] + (coriolis * x[1] - (0.5 * time_step) * gx)
            new[1] = new[1] - (coriolis * x[0] + (0.5 * time_step) * gy)
            for f in (2, 3):
                flux = e[0] * e[f] - w[0] * w[f] + n[1] * n[f] - s[1] * s[f]
                new[f] = new[f] - (0.5 * time_step) * flux
            for f in range(NF):
                done[f, l, r : r + 8, :] = mask * new[f]
        return carry

    for c in range(chunks):
        for f in range(NF):
            load(c, f).wait()
        lax.fori_loop(c * chunk, (c + 1) * chunk, level_step, 0)
        for f in range(NF):
            store(c, f).start()
    for c in range(chunks):
        for f in range(NF):
            store(c, f).wait()


def local(
    zonal_current, meridional_current, warmth_anomaly, brine_anomaly,
    marine_indicator, retained_tile_indicator, seabed_thickness, elevation_pivot_entry,
):
    levels, height, breadth = zonal_current.shape
    n_lon, n_lat = lax.axis_size("lon"), lax.axis_size("lat")
    f32 = jnp.float32
    any_spec = pl.BlockSpec(memory_space=pl.ANY)
    vmem = pl.BlockSpec(memory_space=pltpu.VMEM)
    smem = pl.BlockSpec(memory_space=pltpu.SMEM)
    chunk = 4 if levels % 4 == 0 else 1
    quarters = height // QROWS
    wide = NF * levels + NA * S8
    dma = pltpu.SemaphoreType.DMA
    fields = (zonal_current, meridional_current, warmth_anomaly, brine_anomaly)
    edge, rows, answer, left = pl.pallas_call(
        surface_kernel,
        out_shape=(
            jax.ShapeDtypeStruct((2, height, breadth), f32),
            jax.ShapeDtypeStruct((2, NF, levels, breadth), f32),
            jax.ShapeDtypeStruct((height, breadth), f32),
            jax.ShapeDtypeStruct((height, breadth), f32),
        ),
        in_specs=[any_spec] * 4 + [vmem, smem, vmem, vmem],
        out_specs=(vmem,) * 4,
        scratch_shapes=[
            pltpu.VMEM((NF, levels, height, breadth), f32),
            pltpu.VMEM((2, height, breadth), f32),
            pltpu.VMEM((2, height, breadth), f32),
            pltpu.VMEM((2, wide, breadth), f32),
            pltpu.VMEM((2, height, breadth), f32),
            pltpu.VMEM((2, height, breadth), f32),
            pltpu.VMEM((2, wide, breadth), f32),
            pltpu.VMEM((2, 2, S8, breadth), f32),
            pltpu.VMEM((NA, height + 2 * PAD, 2 * breadth), f32),
            pltpu.VMEM((n_lon, 8, breadth), f32),
            pltpu.VMEM((n_lat, 8, breadth), f32),
            dma((quarters, NF)),
            dma((8,)),
            dma((8,)),
            dma((n_lon - 1,)),
            dma((n_lon - 1,)),
            dma((n_lat - 1,)),
            dma((n_lat - 1,)),
        ],
        compiler_params=pltpu.CompilerParams(
            collective_id=0, has_side_effects=True, vmem_limit_bytes=24 * 2**20
        ),
        name="surface",
    )(*fields, marine_indicator, retained_tile_indicator, seabed_thickness, elevation_pivot_entry)
    new = pl.pallas_call(
        update_kernel,
        out_shape=tuple(jax.ShapeDtypeStruct(x.shape, f32) for x in fields),
        in_specs=[any_spec] * 4 + [vmem] * 3,
        out_specs=(any_spec,) * 4,
        scratch_shapes=[
            pltpu.VMEM((NF, levels, height, breadth), f32),
            pltpu.VMEM((NF, levels, height, breadth), f32),
            pltpu.VMEM((2, NF, height + 2 * PAD, breadth), f32),
            pltpu.VMEM((2, height, breadth), f32),
            dma((levels // chunk, NF)),
            dma((levels // chunk, NF)),
        ],
        compiler_params=pltpu.CompilerParams(vmem_limit_bytes=24 * 2**20),
        name="update",
    )(*fields, marine_indicator, edge, rows)
    return (*new, answer, left)


def solution(mesh):
    cube, flat = P(None, "lat", "lon"), P("lat", "lon")
    return jax.shard_map(
        local,
        mesh=mesh,
        in_specs=(cube,) * 4 + (flat,) * 4,
        out_specs=(cube,) * 4 + (flat,) * 2,
        check_vma=False,
    )
```

time: 367 us -> 49.3 us (0.13)
  blocking collectives: 197 us -> 0 us
  waiting for transfers between devices: 47.1 us -> 0 us
  other arithmetic: 41.4 us -> 0 us
  Pallas kernels: 0 us -> 39 us
  local copies, waits for them, and re-layouts: 46.1 us -> 9.08 us
  starting transfers between devices: 27.1 us -> 0 us
  between operations: 7.74 us -> 0.67 us
    psum x5 -> x0, blocking collectives: 197 us -> none  [the longest x3 121 us: precond_sum(): return lax.psum(jnp.sum(residual * precond), ('lon', 'lat'))]
    ppermute x35 -> x0, waiting for transfers between devices: 47.1 us -> none  [the longest x15 32.5 us: partner(): return lax.ppermute(block, axis, route)]
    pallas_call x0 -> x2, Pallas kernels: none -> 39 us  [the longest x1 24.9 us: local(): pl.pallas_call(surface_kernel, out_shape=(jax.ShapeDtypeStruct((2, height...]
    ppermute x35 -> x0, starting transfers between devices: 27.1 us -> none  [the longest x10 13.5 us: extended(): lax.ppermute(head, axis, [((i + 1) % count, i) for i in range(count)])]
    slice x13 -> x0, local copies, waits for them, and re-layouts: 17 us -> none  [the longest x6 8.71 us: extended(): lax.slice_in_dim(cells, cells.shape[dim] - width, cells.shape[dim], axis=...]
    another operation x5 -> x0, other arithmetic: 16.6 us -> none  [the longest x4 16.6 us: local(): jnp.cumsum(haline * near_s[side] - thermal * near_t[side], axis=0)]
    ppermute x4 -> x0, local copies, waits for them, and re-layouts: 14.1 us -> none  [the longest x2 7.1 us: extended(): lax.ppermute(tail, axis, [(i, (i + 1) % count) for i in range(count)])]
    slice x7 -> x0, other arithmetic: 8.38 us -> none  [the longest x2 6.34 us: pick(): return tuple((item[first:first + count] for item in near))]
  transfers between devices with their start and end apart: 35 -> 0, of which waited for: 19 -> 0; matrix products, arithmetic and copies ran while one was open for 13% -> 0% of each run, Pallas kernels for 0% -> 0%
where the time goes in v1:
time: 49.3 us; the launch traced here: 48.8 us
  Pallas kernels  39 us (79%)
  local copies, waits for them, and re-layouts  9.08 us (18%)
  between operations  0.67 us (1%)
    pallas_call x1, Pallas kernels, local(): pl.pallas_call(surface_kernel, out_shape=(jax.ShapeDtypeStruct((2, height...  24.9 us
    pallas_call x1, Pallas kernels, local(): pl.pallas_call(update_kernel, out_shape=tuple((jax.ShapeDtypeStruct(x.sha...  14.1 us
    unnamed x18, local copies, waits for them, and re-layouts  9.08 us

profile of v1, /device:TPU:0, one launch (start us, length us, event | category | flops | bytes accessed | tf_op | source)
XLA Modules:
  0.0 48.8 jit_solution(5730776569045724949)
XLA Ops:
  0.6 0.0 copy-start
  0.6 1.2 %copy-done = f32[32,64,128]{2,1,0:T(8,128)S(1)} copy-done((f32[32,64,128]{2,1,0:T(8,128)S(1)}, f32[32,64,128]{2,1,0:T(8,128)}, u32[]{:S(2)}) %copy-start) | copy-done | bytes 1048600
  1.9 0.0 copy-start.1
  1.9 1.2 %copy-done.1 = f32[32,64,128]{2,1,0:T(8,128)S(1)} copy-done((f32[32,64,128]{2,1,0:T(8,128)S(1)}, f32[32,64,128]{2,1,0:T(8,128)}, u32[]{:S(2)}) %copy-start.1) | copy-done | bytes 1048600
  3.1 0.0 copy-start.2
  3.1 1.2 %copy-done.2 = f32[32,64,128]{2,1,0:T(8,128)S(1)} copy-done((f32[32,64,128]{2,1,0:T(8,128)S(1)}, f32[32,64,128]{2,1,0:T(8,128)}, u32[]{:S(2)}) %copy-start.2) | copy-done | bytes 1048600
  4.3 0.0 copy-start.3
  4.3 1.2 %copy-done.3 = f32[32,64,128]{2,1,0:T(8,128)S(1)} copy-done((f32[32,64,128]{2,1,0:T(8,128)S(1)}, f32[32,64,128]{2,1,0:T(8,128)}, u32[]{:S(2)}) %copy-start.3) | copy-done | bytes 1048600
  5.5 0.0 copy-start.4
  5.5 0.8 %copy-done.4 = s32[64,128]{1,0:T(8,128)S(1)} copy-done((s32[64,128]{1,0:T(8,128)S(1)}, s32[64,128]{1,0:T(8,128)}, u32[]{:S(2)}) %copy-start.4) | copy-done | bytes 32792
  6.3 0.0 copy-start.5
  6.3 0.8 %copy-done.5 = f32[64,128]{1,0:T(8,128)S(1)} copy-done((f32[64,128]{1,0:T(8,128)S(1)}, f32[64,128]{1,0:T(8,128)}, u32[]{:S(2)}) %copy-start.5) | copy-done | bytes 32792
  7.1 0.0 copy-start.6
  7.1 0.8 %copy-done.6 = f32[64,128]{1,0:T(8,128)S(1)} copy-done((f32[64,128]{1,0:T(8,128)S(1)}, f32[64,128]{1,0:T(8,128)}, u32[]{:S(2)}) %copy-start.6) | copy-done | bytes 32792
  7.8 0.0 copy-start.7
  7.8 0.7 %copy-done.7 = s32[4,8]{1,0:T(4,128)S(1)} copy-done((s32[4,8]{1,0:T(4,128)S(1)}, s32[4,8]{1,0:T(4,128)}, u32[]{:S(2)}) %copy-start.7) | copy-done | bytes 152
  8.5 24.9 %surface.1 = (f32[2,64,128]{2,1,0:T(8,128)S(1)}, f32[2,4,32,128]{3,2,1,0:T(8,128)S(1)}, f32[64,128]{1,0:T(8,128)S(1)}, f32[64,128]{1,0:T(8,128)S(1)}) custom-call(f32[32,64,128]{2,1,0:T(8,128)S(1)} %copy-done, f32[32,64,128]{2,1,0:T(8,128)S(1)} %copy-done.1, f32[32,64,128]{2,1,0:T(8,128)S(1)} %copy-done.2, f32[32,64,128]{2,1,0:T(8,128)S(1)} %copy-done.3, ...), custom_call_target="tpu_custom_call" | custom-call | tf_op jit(solution)/shard_map/surface/pallas_call | solution.py:499
  33.4 14.1 %update.1 = (f32[32,64,128]{2,1,0:T(8,128)}, f32[32,64,128]{2,1,0:T(8,128)}, f32[32,64,128]{2,1,0:T(8,128)}, f32[32,64,128]{2,1,0:T(8,128)}) custom-call(f32[32,64,128]{2,1,0:T(8,128)S(1)} %copy-done, f32[32,64,128]{2,1,0:T(8,128)S(1)} %copy-done.1, f32[32,64,128]{2,1,0:T(8,128)S(1)} %copy-done.2, f32[32,64,128]{2,1,0:T(8,128)S(1)} %copy-done.3, ...), custom_call_target="tpu_custom_call" | custom-call | tf_op jit(solution)/shard_map/update/pallas_call | solution.py:534
  47.5 0.6 %copy.16 = f32[64,128]{1,0:T(8,128)} copy(f32[64,128]{1,0:T(8,128)S(1)} %get-tuple-element.32) | data formatting | bytes 65536
  48.1 0.6 %copy.17 = f32[64,128]{1,0:T(8,128)} copy(f32[64,128]{1,0:T(8,128)S(1)} %get-tuple-element.33) | data formatting | bytes 65536
Async XLA Ops:
  0.6 1.2 %copy-start = (f32[32,64,128]{2,1,0:T(8,128)S(1)}, f32[32,64,128]{2,1,0:T(8,128)}, u32[]{:S(2)}) copy-start(f32[32,64,128]{2,1,0:T(8,128)} %u_ref.3) | copy-start | bytes 3145732
  1.9 1.2 %copy-start.1 = (f32[32,64,128]{2,1,0:T(8,128)S(1)}, f32[32,64,128]{2,1,0:T(8,128)}, u32[]{:S(2)}) copy-start(f32[32,64,128]{2,1,0:T(8,128)} %v_ref.3) | copy-start | bytes 3145732
  3.1 1.2 %copy-start.2 = (f32[32,64,128]{2,1,0:T(8,128)S(1)}, f32[32,64,128]{2,1,0:T(8,128)}, u32[]{:S(2)}) copy-start(f32[32,64,128]{2,1,0:T(8,128)} %t_ref.3) | copy-start | bytes 3145732
  4.3 1.2 %copy-start.3 = (f32[32,64,128]{2,1,0:T(8,128)S(1)}, f32[32,64,128]{2,1,0:T(8,128)}, u32[]{:S(2)}) copy-start(f32[32,64,128]{2,1,0:T(8,128)} %s_ref.3) | copy-start | bytes 3145732
  5.5 0.8 %copy-start.4 = (s32[64,128]{1,0:T(8,128)S(1)}, s32[64,128]{1,0:T(8,128)}, u32[]{:S(2)}) copy-start(s32[64,128]{1,0:T(8,128)} %marine_ref.3) | copy-start | bytes 98308
  6.3 0.8 %copy-start.5 = (f32[64,128]{1,0:T(8,128)S(1)}, f32[64,128]{1,0:T(8,128)}, u32[]{:S(2)}) copy-start(f32[64,128]{1,0:T(8,128)} %depth_ref.1) | copy-start | bytes 98308
  7.1 0.8 %copy-start.6 = (f32[64,128]{1,0:T(8,128)S(1)}, f32[64,128]{1,0:T(8,128)}, u32[]{:S(2)}) copy-start(f32[64,128]{1,0:T(8,128)} %elev_ref.1) | copy-start | bytes 98308
  7.8 0.7 %copy-start.7 = (s32[4,8]{1,0:T(4,128)S(1)}, s32[4,8]{1,0:T(4,128)}, u32[]{:S(2)}) copy-start(s32[4,8]{1,0:T(4,128)} %kept_ref.1) | copy-start | bytes 388

commit v2 on v1

--- a/solution.py
+++ b/solution.py
@@ -21,7 +21,7 @@
 NA = 6
 STRIP = 16
 S8 = 8
-QROWS = 16
+QROWS = 32
 PAD = 8
 
 
@@ -39,10 +39,10 @@
 
 
 def surface_kernel(
-    u_ref, v_ref, t_ref, s_ref, marine_ref, kept_ref, depth_ref, elev_ref,
+    u_ref, v_ref, t_ref, s_ref, marine_hbm, kept_hbm, depth_hbm, elev_hbm,
     edge_ref, rows_ref, sol_ref, res_ref,
     held, send_e, send_w, send_v, recv_e, recv_w, recv_v, recv_c, ext,
-    part_lon, part_lat, load_sem, send_sem, recv_sem, lon_send, lon_recv, lat_send, lat_recv,
+    part_lon, part_lat, marine_ref, kept_ref, depth_ref, elev_ref, flat_sem, load_sem, send_sem, recv_sem, lon_send, lon_recv, lat_send, lat_recv,
 ):
     n_lon, n_lat = lax.axis_size("lon"), lax.axis_size("lat")
     lon, lat = lax.axis_index("lon"), lax.axis_index("lat")
@@ -51,6 +51,14 @@
     east, west = lax.rem(lon + 1, n_lon), lax.rem(lon + n_lon - 1, n_lon)
     mirror = n_lon - 1 - lon
 
+    flat = [
+        pltpu.make_async_copy(src, dst, flat_sem.at[i])
+        for i, (src, dst) in enumerate(
+            ((marine_hbm, marine_ref), (kept_hbm, kept_ref), (depth_hbm, depth_ref), (elev_hbm, elev_ref))
+        )
+    ]
+    for copy in flat:
+        copy.start()
     fields = (u_ref, v_ref, t_ref, s_ref)
     quarters = height // QROWS
     loads = []
@@ -88,6 +96,8 @@
         greet(east, lat + 1)
         greet(west, lat + 1)
 
+    for copy in flat:
+        copy.wait()
     lane = lax.broadcasted_iota(jnp.int32, (height, breadth), 1)
     ocean = marine_ref[...].astype(jnp.float32)
     bands = []
@@ -399,9 +409,9 @@
 
 
 def update_kernel(
-    u_ref, v_ref, t_ref, s_ref, marine_ref, edge_ref, rows_ref,
-    u_out, v_out, t_out, s_out,
-    held, done, padded, slope, load_sem, store_sem,
+    u_ref, v_ref, t_ref, s_ref, marine_hbm, edge_ref, rows_ref, answer_ref, left_ref,
+    u_out, v_out, t_out, s_out, answer_out, left_out,
+    held, done, padded, slope, marine_ref, load_sem, store_sem, flat_sem,
 ):
     lat = lax.axis_index("lat")
     levels, height, breadth = u_ref.shape
@@ -417,15 +427,26 @@
         part = pl.ds(c * chunk, chunk)
         return pltpu.make_async_copy(done.at[f, part], outs[f].at[part], store_sem.at[c, f])
 
+    flat = [
+        pltpu.make_async_copy(src, dst, flat_sem.at[i])
+        for i, (src, dst) in enumerate(
+            ((marine_hbm, marine_ref), (answer_ref, answer_out), (left_ref, left_out))
+        )
+    ]
+    flat[0].start()
     for c in range(chunks):
         for f in range(NF):
             load(c, f).start()
+    flat[1].start()
+    flat[2].start()
     slope[...] = jnp.zeros_like(slope)
     total_rows = lax.axis_size("lat") * height
     lane = lax.broadcasted_iota(jnp.int32, (8, breadth), 1)
     first_lane, last_lane = lane == 0, lane == breadth - 1
     row8 = lax.broadcasted_iota(jnp.int32, (8, breadth), 0)
     mul_q = (time_step * viscosity, time_step * viscosity, time_step * diffusivity, time_step * diffusivity)
+
+    flat[0].wait()
 
     def level_step(l, carry):
         b = lax.rem(l, 2)
@@ -479,6 +500,8 @@
     for c in range(chunks):
         for f in range(NF):
             store(c, f).wait()
+    flat[1].wait()
+    flat[2].wait()
 
 
 def local(
@@ -488,9 +511,8 @@
     levels, height, breadth = zonal_current.shape
     n_lon, n_lat = lax.axis_size("lon"), lax.axis_size("lat")
     f32 = jnp.float32
-    any_spec = pl.BlockSpec(memory_space=pl.ANY)
     vmem = pl.BlockSpec(memory_space=pltpu.VMEM)
-    smem = pl.BlockSpec(memory_space=pltpu.SMEM)
+    hbm = pl.BlockSpec(memory_space=pltpu.HBM)
     chunk = 4 if levels % 4 == 0 else 1
     quarters = height // QROWS
     wide = NF * levels + NA * S8
@@ -504,7 +526,7 @@
             jax.ShapeDtypeStruct((height, breadth), f32),
             jax.ShapeDtypeStruct((height, breadth), f32),
         ),
-        in_specs=[any_spec] * 4 + [vmem, smem, vmem, vmem],
+        in_specs=[hbm] * 8,
         out_specs=(vmem,) * 4,
         scratch_shapes=[
             pltpu.VMEM((NF, levels, height, breadth), f32),
@@ -518,6 +540,11 @@
             pltpu.VMEM((NA, height + 2 * PAD, 2 * breadth), f32),
             pltpu.VMEM((n_lon, 8, breadth), f32),
             pltpu.VMEM((n_lat, 8, breadth), f32),
+            pltpu.VMEM((height, breadth), jnp.int32),
+            pltpu.SMEM(retained_tile_indicator.shape, jnp.int32),
+            pltpu.VMEM((height, breadth), f32),
+            pltpu.VMEM((height, breadth), f32),
+            dma((4,)),
             dma((quarters, NF)),
             dma((8,)),
             dma((8,)),
@@ -527,27 +554,29 @@
             dma((n_lat - 1,)),
         ],
         compiler_params=pltpu.CompilerParams(
-            collective_id=0, has_side_effects=True, vmem_limit_bytes=24 * 2**20
+            collective_id=0, has_side_effects=True, vmem_limit_bytes=60 * 2**20
         ),
         name="surface",
     )(*fields, marine_indicator, retained_tile_indicator, seabed_thickness, elevation_pivot_entry)
     new = pl.pallas_call(
         update_kernel,
-        out_shape=tuple(jax.ShapeDtypeStruct(x.shape, f32) for x in fields),
-        in_specs=[any_spec] * 4 + [vmem] * 3,
-        out_specs=(any_spec,) * 4,
+        out_shape=tuple(jax.ShapeDtypeStruct(x.shape, f32) for x in (*fields, answer, left)),
+        in_specs=[hbm] * 5 + [vmem] * 2 + [hbm] * 2,
+        out_specs=(hbm,) * 6,
         scratch_shapes=[
             pltpu.VMEM((NF, levels, height, breadth), f32),
             pltpu.VMEM((NF, levels, height, breadth), f32),
             pltpu.VMEM((2, NF, height + 2 * PAD, breadth), f32),
             pltpu.VMEM((2, height, breadth), f32),
+            pltpu.VMEM((height, breadth), jnp.int32),
             dma((levels // chunk, NF)),
             dma((levels // chunk, NF)),
+            dma((3,)),
         ],
-        compiler_params=pltpu.CompilerParams(vmem_limit_bytes=24 * 2**20),
+        compiler_params=pltpu.CompilerParams(vmem_limit_bytes=60 * 2**20),
         name="update",
-    )(*fields, marine_indicator, edge, rows)
-    return (*new, answer, left)
+    )(*fields, marine_indicator, edge, rows, answer, left)
+    return new
 
 
 def solution(mesh):

time: 49.3 us -> 36.7 us (0.74)
  local copies, waits for them, and re-layouts: 9.08 us -> 0 us
  Pallas kernels: 39 us -> 35.9 us
    unnamed x18 -> x0, local copies, waits for them, and re-layouts: 9.08 us -> none
    pallas_call x1, Pallas kernels: 14.1 us -> 11.7 us  [local(): pl.pallas_call(update_kernel, out_shape=tuple((jax.ShapeDtypeStruct(x.sha...]
    pallas_call x1, Pallas kernels: 24.9 us -> 24.2 us  [local(): pl.pallas_call(surface_kernel, out_shape=(jax.ShapeDtypeStruct((2, height...]
where the time goes in v2:
time: 36.7 us; the launch traced here: 36.5 us
  Pallas kernels  35.9 us (98%)
  between operations  0.64 us (2%)
    pallas_call x1, Pallas kernels, local(): pl.pallas_call(surface_kernel, out_shape=(jax.ShapeDtypeStruct((2, height...  24.2 us
    pallas_call x1, Pallas kernels, local(): pl.pallas_call(update_kernel, out_shape=tuple((jax.ShapeDtypeStruct(x.sha...  11.7 us

profile of v2, /device:TPU:0, one launch (start us, length us, event | category | flops | bytes accessed | tf_op | source)
XLA Modules:
  0.0 36.5 jit_solution(16428069343613152264)
XLA Ops:
  0.6 24.2 %surface.1 = (f32[2,64,128]{2,1,0:T(8,128)}, f32[2,4,32,128]{3,2,1,0:T(8,128)}, f32[64,128]{1,0:T(8,128)}, f32[64,128]{1,0:T(8,128)}) custom-call(f32[32,64,128]{2,1,0:T(8,128)} %u_ref.3, f32[32,64,128]{2,1,0:T(8,128)} %v_ref.3, f32[32,64,128]{2,1,0:T(8,128)} %t_ref.3, f32[32,64,128]{2,1,0:T(8,128)} %s_ref.3, s32[64,128]{1,0:T(8,128)} %marine_hbm.3, ...), custom_call_target="tpu_custom_call" | custom-call | tf_op jit(solution)/shard_map/surface/pallas_call | solution.py:521
  24.9 11.7 %update.1 = (f32[32,64,128]{2,1,0:T(8,128)}, f32[32,64,128]{2,1,0:T(8,128)}, f32[32,64,128]{2,1,0:T(8,128)}, f32[32,64,128]{2,1,0:T(8,128)}, f32[64,128]{1,0:T(8,128)}, /*index=5*/f32[64,128]{1,0:T(8,128)}) custom-call(f32[32,64,128]{2,1,0:T(8,128)} %u_ref.3, f32[32,64,128]{2,1,0:T(8,128)} %v_ref.3, f32[32,64,128]{2,1,0:T(8,128)} %t_ref.3, ...), custom_call_target="tpu_custom_call" | custom-call | tf_op jit(solution)/shard_map/update/pallas_call | solution.py:561

commit v3 on v2

--- a/solution.py
+++ b/solution.py
@@ -40,8 +40,8 @@
 
 def surface_kernel(
     u_ref, v_ref, t_ref, s_ref, marine_hbm, kept_hbm, depth_hbm, elev_hbm,
-    edge_ref, rows_ref, sol_ref, res_ref,
-    held, send_e, send_w, send_v, recv_e, recv_w, recv_v, recv_c, ext,
+    u_mid, v_mid, t_mid, s_mid_, sol_ref, res_ref,
+    edge_ref, rows_ref, done, padded, slope, store_sem, held, send_e, send_w, send_v, recv_e, recv_w, recv_v, recv_c, ext,
     part_lon, part_lat, marine_ref, kept_ref, depth_ref, elev_ref, flat_sem, load_sem, send_sem, recv_sem, lon_send, lon_recv, lat_send, lat_recv,
 ):
     n_lon, n_lat = lax.axis_size("lon"), lax.axis_size("lat")
@@ -327,7 +327,7 @@
         moments.append(jnp.zeros((1, breadth), jnp.float32))
     tile = jnp.concatenate(moments, axis=0)
 
-    def gather_sum(tile, parts, me, n, sends, recvs, axis):
+    def send_parts(tile, parts, me, n, sends, recvs, axis):
         parts[me] = tile
         copies = []
         for o in range(1, n):
@@ -339,6 +339,9 @@
             )
             copy.start()
             copies.append(copy)
+        return copies
+
+    def sum_parts(parts, me, n, sends, recvs, axis):
         for o in range(1, n):
             source = lax.rem(me + n - o, n)
             pltpu.make_async_remote_copy(
@@ -349,106 +352,19 @@
         total = parts[0]
         for i in range(1, n):
             total = total + parts[i]
-        return total, copies
-
-    tile, lon_copies = gather_sum(tile, part_lon, lon, n_lon, lon_send, lon_recv, "lon")
-    tile, lat_copies = gather_sum(tile, part_lat, lat, n_lat, lat_send, lat_recv, "lat")
-    sums = jnp.broadcast_to(jnp.sum(tile, axis=1, keepdims=True), tile.shape)
-    m = [sums[i : i + 1, :] for i in range(2 * ITERS)]
-
-    def dot(a, b):
-        total = 0.0
-        for i, p in enumerate(a):
-            for j, q in enumerate(b):
-                total = total + (p * q) * m[i + j]
         return total
 
-    one = jnp.ones((1, breadth), jnp.float32)
-    z, d = [one], [one]
-    x = []
-    rz = m[0]
-    for step in range(ITERS):
-        image = [d[0]] + [d[i] - d[i - 1] for i in range(1, len(d))] + [-d[-1]]
-        alpha = rz / dot(d, image)
-        x = [alpha * d[i] + (x[i] if i < len(x) else 0.0) for i in range(len(d))]
-        z = [(z[i] if i < len(z) else 0.0) - alpha * image[i] for i in range(len(image))]
-        if step + 1 < ITERS:
-            rz_new = dot(z, z)
-            beta = rz_new / rz
-            d = [z[i] + (beta * d[i] if i < len(d) else 0.0) for i in range(len(z))]
-            rz = rz_new
-    answer = x[0] * inner[0]
-    for i in range(1, ITERS):
-        answer = answer + x[i] * inner[i]
-    left = z[0] * weighted[0]
-    for i in range(1, ITERS + 1):
-        left = left + z[i] * weighted[i]
-    sol_ref[...] = answer
-    res_ref[...] = left
-
-    go_up.wait_send()
-    go_e.wait_send()
-    go_w.wait_send()
-
-    @pl.when(lat > 0)
-    def _():
-        go_down.wait_send()
-        go_down_e.wait_send()
-        go_down_w.wait_send()
-
-    @pl.when(jnp.logical_not(self_e))
-    def _():
-        go_up_e.wait_send()
-
-    @pl.when(jnp.logical_not(self_w))
-    def _():
-        go_up_w.wait_send()
-
-    for copy in lon_copies + lat_copies:
-        copy.wait_send()
-
-
-def update_kernel(
-    u_ref, v_ref, t_ref, s_ref, marine_hbm, edge_ref, rows_ref, answer_ref, left_ref,
-    u_out, v_out, t_out, s_out, answer_out, left_out,
-    held, done, padded, slope, marine_ref, load_sem, store_sem, flat_sem,
-):
-    lat = lax.axis_index("lat")
-    levels, height, breadth = u_ref.shape
-    fields, outs = (u_ref, v_ref, t_ref, s_ref), (u_out, v_out, t_out, s_out)
-    chunk = 4 if levels % 4 == 0 else 1
+    lon_copies = send_parts(tile, part_lon, lon, n_lon, lon_send, lon_recv, "lon")
+    chunk = 8 if levels % 8 == 0 else 1
     chunks = levels // chunk
-
-    def load(c, f):
-        part = pl.ds(c * chunk, chunk)
-        return pltpu.make_async_copy(fields[f].at[part], held.at[f, part], load_sem.at[c, f])
-
-    def store(c, f):
-        part = pl.ds(c * chunk, chunk)
-        return pltpu.make_async_copy(done.at[f, part], outs[f].at[part], store_sem.at[c, f])
-
-    flat = [
-        pltpu.make_async_copy(src, dst, flat_sem.at[i])
-        for i, (src, dst) in enumerate(
-            ((marine_hbm, marine_ref), (answer_ref, answer_out), (left_ref, left_out))
-        )
-    ]
-    flat[0].start()
-    for c in range(chunks):
-        for f in range(NF):
-            load(c, f).start()
-    flat[1].start()
-    flat[2].start()
+    mids = (u_mid, v_mid, t_mid, s_mid_)
     slope[...] = jnp.zeros_like(slope)
-    total_rows = lax.axis_size("lat") * height
-    lane = lax.broadcasted_iota(jnp.int32, (8, breadth), 1)
-    first_lane, last_lane = lane == 0, lane == breadth - 1
+    lane8 = lax.broadcasted_iota(jnp.int32, (8, breadth), 1)
+    first_lane, last_lane = lane8 == 0, lane8 == breadth - 1
     row8 = lax.broadcasted_iota(jnp.int32, (8, breadth), 0)
-    mul_q = (time_step * viscosity, time_step * viscosity, time_step * diffusivity, time_step * diffusivity)
-
-    flat[0].wait()
-
-    def level_step(l, carry):
+    mul_q = (time_step * viscosity,) * 2 + (time_step * diffusivity,) * 2
+
+    def update_step(l, carry):
         b = lax.rem(l, 2)
         for f in range(NF):
             padded[b, f, PAD - 1 : PAD, :] = rows_ref[0, f, pl.ds(l, 1), :]
@@ -491,17 +407,91 @@
                 done[f, l, r : r + 8, :] = mask * new[f]
         return carry
 
-    for c in range(chunks):
-        for f in range(NF):
-            load(c, f).wait()
-        lax.fori_loop(c * chunk, (c + 1) * chunk, level_step, 0)
-        for f in range(NF):
-            store(c, f).start()
-    for c in range(chunks):
-        for f in range(NF):
-            store(c, f).wait()
-    flat[1].wait()
-    flat[2].wait()
+    stores = []
+
+    def update(low, high):
+        for c in range(low, high):
+            lax.fori_loop(c * chunk, (c + 1) * chunk, update_step, 0)
+            part = pl.ds(c * chunk, chunk)
+            for f in range(NF):
+                copy = pltpu.make_async_copy(
+                    done.at[f, part], mids[f].at[part], store_sem.at[c, f]
+                )
+                copy.start()
+                stores.append(copy)
+
+    update(0, chunks // 2)
+    tile = sum_parts(part_lon, lon, n_lon, lon_send, lon_recv, "lon")
+    lat_copies = send_parts(tile, part_lat, lat, n_lat, lat_send, lat_recv, "lat")
+    update(chunks // 2, chunks)
+    tile = sum_parts(part_lat, lat, n_lat, lat_send, lat_recv, "lat")
+    sums = jnp.broadcast_to(jnp.sum(tile, axis=1, keepdims=True), tile.shape)
+    m = [sums[i : i + 1, :] for i in range(2 * ITERS)]
+
+    def dot(a, b):
+        total = 0.0
+        for i, p in enumerate(a):
+            for j, q in enumerate(b):
+                total = total + (p * q) * m[i + j]
+        return total
+
+    one = jnp.ones((1, breadth), jnp.float32)
+    z, d = [one], [one]
+    x = []
+    rz = m[0]
+    for step in range(ITERS):
+        image = [d[0]] + [d[i] - d[i - 1] for i in range(1, len(d))] + [-d[-1]]
+        alpha = rz / dot(d, image)
+        x = [alpha * d[i] + (x[i] if i < len(x) else 0.0) for i in range(len(d))]
+        z = [(z[i] if i < len(z) else 0.0) - alpha * image[i] for i in range(len(image))]
+        if step + 1 < ITERS:
+            rz_new = dot(z, z)
+            beta = rz_new / rz
+            d = [z[i] + (beta * d[i] if i < len(d) else 0.0) for i in range(len(z))]
+            rz = rz_new
+    answer = x[0] * inner[0]
+    for i in range(1, ITERS):
+        answer = answer + x[i] * inner[i]
+    left = z[0] * weighted[0]
+    for i in range(1, ITERS + 1):
+        left = left + z[i] * weighted[i]
+    sol_ref[...] = answer
+    res_ref[...] = left
+
+    go_up.wait_send()
+    go_e.wait_send()
+    go_w.wait_send()
+
+    @pl.when(lat > 0)
+    def _():
+        go_down.wait_send()
+        go_down_e.wait_send()
+        go_down_w.wait_send()
+
+    @pl.when(jnp.logical_not(self_e))
+    def _():
+        go_up_e.wait_send()
+
+    @pl.when(jnp.logical_not(self_w))
+    def _():
+        go_up_w.wait_send()
+
+    for copy in lon_copies + lat_copies:
+        copy.wait_send()
+    for copy in stores:
+        copy.wait()
+
+
+def place_kernel(*refs):
+    *arrays, sem = refs
+    half = len(arrays) // 2
+    copies = [
+        pltpu.make_async_copy(arrays[i], arrays[half + i], sem.at[i]) for i in range(half)
+    ]
+    for copy in copies:
+        copy.start()
+    for copy in copies:
+        copy.wait()
 
 
 def local(
@@ -513,22 +503,24 @@
     f32 = jnp.float32
     vmem = pl.BlockSpec(memory_space=pltpu.VMEM)
     hbm = pl.BlockSpec(memory_space=pltpu.HBM)
-    chunk = 4 if levels % 4 == 0 else 1
+    chunk = 8 if levels % 8 == 0 else 1
     quarters = height // QROWS
     wide = NF * levels + NA * S8
     dma = pltpu.SemaphoreType.DMA
     fields = (zonal_current, meridional_current, warmth_anomaly, brine_anomaly)
-    edge, rows, answer, left = pl.pallas_call(
+    results = tuple(jax.ShapeDtypeStruct(x.shape, f32) for x in (*fields, seabed_thickness, seabed_thickness))
+    middle = pl.pallas_call(
         surface_kernel,
-        out_shape=(
-            jax.ShapeDtypeStruct((2, height, breadth), f32),
-            jax.ShapeDtypeStruct((2, NF, levels, breadth), f32),
-            jax.ShapeDtypeStruct((height, breadth), f32),
-            jax.ShapeDtypeStruct((height, breadth), f32),
-        ),
+        out_shape=results,
         in_specs=[hbm] * 8,
-        out_specs=(vmem,) * 4,
+        out_specs=(hbm,) * 4 + (vmem,) * 2,
         scratch_shapes=[
+            pltpu.VMEM((2, height, breadth), f32),
+            pltpu.VMEM((2, NF, levels, breadth), f32),
+            pltpu.VMEM((NF, levels, height, breadth), f32),
+            pltpu.VMEM((2, NF, height + 2 * PAD, breadth), f32),
+            pltpu.VMEM((2, height, breadth), f32),
+            dma((levels // chunk, NF)),
             pltpu.VMEM((NF, levels, height, breadth), f32),
             pltpu.VMEM((2, height, breadth), f32),
             pltpu.VMEM((2, height, breadth), f32),
@@ -558,25 +550,15 @@
         ),
         name="surface",
     )(*fields, marine_indicator, retained_tile_indicator, seabed_thickness, elevation_pivot_entry)
-    new = pl.pallas_call(
-        update_kernel,
-        out_shape=tuple(jax.ShapeDtypeStruct(x.shape, f32) for x in (*fields, answer, left)),
-        in_specs=[hbm] * 5 + [vmem] * 2 + [hbm] * 2,
+    return pl.pallas_call(
+        place_kernel,
+        out_shape=results,
+        in_specs=[hbm] * 6,
         out_specs=(hbm,) * 6,
-        scratch_shapes=[
-            pltpu.VMEM((NF, levels, height, breadth), f32),
-            pltpu.VMEM((NF, levels, height, breadth), f32),
-            pltpu.VMEM((2, NF, height + 2 * PAD, breadth), f32),
-            pltpu.VMEM((2, height, breadth), f32),
-            pltpu.VMEM((height, breadth), jnp.int32),
-            dma((levels // chunk, NF)),
-            dma((levels // chunk, NF)),
-            dma((3,)),
-        ],
+        scratch_shapes=[dma((6,))],
         compiler_params=pltpu.CompilerParams(vmem_limit_bytes=60 * 2**20),
-        name="update",
-    )(*fields, marine_indicator, edge, rows, answer, left)
-    return new
+        name="place",
+    )(*middle)
 
 
 def solution(mesh):

time: 36.7 us -> 156 us (4.25)
  Pallas kernels: 35.9 us -> 155 us
    pallas_call x2, Pallas kernels: 35.9 us -> 155 us  [the longest x1 130 us: local(): pl.pallas_call(place_kernel, out_shape=results, in_specs=[hbm] * 6, out_s...]
where the time goes in v3:
time: 156 us
  Pallas kernels  155 us (99%)
    pallas_call x1, Pallas kernels, local(): pl.pallas_call(place_kernel, out_shape=results, in_specs=[hbm] * 6, out_s...  130 us
    pallas_call x1, Pallas kernels, local(): pl.pallas_call(surface_kernel, out_shape=results, in_specs=[hbm] * 8, out...  25.1 us

profile of v3, /device:TPU:0, one launch (start us, length us, event | category | flops | bytes accessed | tf_op | source)
XLA Modules:
  0.0 155.9 jit_solution(1688121055769096046)
XLA Ops:
  0.6 25.1 %surface.1 = (f32[32,64,128]{2,1,0:T(8,128)}, f32[32,64,128]{2,1,0:T(8,128)}, f32[32,64,128]{2,1,0:T(8,128)}, f32[32,64,128]{2,1,0:T(8,128)}, f32[64,128]{1,0:T(8,128)}, /*index=5*/f32[64,128]{1,0:T(8,128)}) custom-call(f32[32,64,128]{2,1,0:T(8,128)} %u_ref.1, f32[32,64,128]{2,1,0:T(8,128)} %v_ref.1, f32[32,64,128]{2,1,0:T(8,128)} %t_ref.1, ...), custom_call_target="tpu_custom_call" | custom-call | tf_op jit(solution)/shard_map/surface/pallas_call | solution.py:512
  25.7 130.2 %place.1 = (f32[32,64,128]{2,1,0:T(8,128)}, f32[32,64,128]{2,1,0:T(8,128)}, f32[32,64,128]{2,1,0:T(8,128)}, f32[32,64,128]{2,1,0:T(8,128)}, f32[64,128]{1,0:T(8,128)}, /*index=5*/f32[64,128]{1,0:T(8,128)}) custom-call(f32[32,64,128]{2,1,0:T(8,128)} %get-tuple-element.12.refs_0_, f32[32,64,128]{2,1,0:T(8,128)} %get-tuple-element.13.refs_1_, ...), custom_call_target="tpu_custom_call" | custom-call | tf_op jit(solution)/shard_map/place/pallas_call | solution.py:553

commit v4 on v3

--- a/solution.py
+++ b/solution.py
@@ -483,15 +483,30 @@
 
 
 def place_kernel(*refs):
-    *arrays, sem = refs
-    half = len(arrays) // 2
-    copies = [
-        pltpu.make_async_copy(arrays[i], arrays[half + i], sem.at[i]) for i in range(half)
-    ]
-    for copy in copies:
-        copy.start()
-    for copy in copies:
-        copy.wait()
+    arrays, held, flat, load_sem, store_sem, flat_load, flat_store = refs[:12], *refs[12:]
+    levels = arrays[0].shape[0]
+    chunk = 8 if levels % 8 == 0 else 1
+    moves = []
+    for c in range(levels // chunk):
+        part = pl.ds(c * chunk, chunk)
+        for f in range(NF):
+            slot = held.at[f, part]
+            moves.append((
+                pltpu.make_async_copy(arrays[f].at[part], slot, load_sem.at[c, f]),
+                pltpu.make_async_copy(slot, arrays[6 + f].at[part], store_sem.at[c, f]),
+            ))
+    for i in range(2):
+        moves.append((
+            pltpu.make_async_copy(arrays[4 + i], flat.at[i], flat_load.at[i]),
+            pltpu.make_async_copy(flat.at[i], arrays[10 + i], flat_store.at[i]),
+        ))
+    for load, _ in moves:
+        load.start()
+    for load, store in moves:
+        load.wait()
+        store.start()
+    for _, store in moves:
+        store.wait()
 
 
 def local(
@@ -555,7 +570,14 @@
         out_shape=results,
         in_specs=[hbm] * 6,
         out_specs=(hbm,) * 6,
-        scratch_shapes=[dma((6,))],
+        scratch_shapes=[
+            pltpu.VMEM((NF, levels, height, breadth), f32),
+            pltpu.VMEM((2, height, breadth), f32),
+            dma((levels // chunk, NF)),
+            dma((levels // chunk, NF)),
+            dma((2,)),
+            dma((2,)),
+        ],
         compiler_params=pltpu.CompilerParams(vmem_limit_bytes=60 * 2**20),
         name="place",
     )(*middle)

time: 156 us -> 29.8 us (0.19)
  Pallas kernels: 155 us -> 29 us
    pallas_call x1, Pallas kernels: 130 us -> 3.93 us  [local(): pl.pallas_call(place_kernel, out_shape=results, in_specs=[hbm] * 6, out_s...]
where the time goes in v4:
time: 29.8 us; the launch traced here: 29.6 us
  Pallas kernels  29 us (97%)
  between operations  0.64 us (2%)
    pallas_call x1, Pallas kernels, local(): pl.pallas_call(surface_kernel, out_shape=results, in_specs=[hbm] * 8, out...  25.1 us
    pallas_call x1, Pallas kernels, local(): pl.pallas_call(place_kernel, out_shape=results, in_specs=[hbm] * 6, out_s...  3.93 us

profile of v4, /device:TPU:0, one launch (start us, length us, event | category | flops | bytes accessed | tf_op | source)
XLA Modules:
  0.0 29.6 jit_solution(17839294963108454658)
XLA Ops:
  0.6 25.1 %surface.1 = (f32[32,64,128]{2,1,0:T(8,128)}, f32[32,64,128]{2,1,0:T(8,128)}, f32[32,64,128]{2,1,0:T(8,128)}, f32[32,64,128]{2,1,0:T(8,128)}, f32[64,128]{1,0:T(8,128)}, /*index=5*/f32[64,128]{1,0:T(8,128)}) custom-call(f32[32,64,128]{2,1,0:T(8,128)} %u_ref.1, f32[32,64,128]{2,1,0:T(8,128)} %v_ref.1, f32[32,64,128]{2,1,0:T(8,128)} %t_ref.1, ...), custom_call_target="tpu_custom_call" | custom-call | tf_op jit(solution)/shard_map/surface/pallas_call | solution.py:527
  25.7 3.9 %place.1 = (f32[32,64,128]{2,1,0:T(8,128)}, f32[32,64,128]{2,1,0:T(8,128)}, f32[32,64,128]{2,1,0:T(8,128)}, f32[32,64,128]{2,1,0:T(8,128)}, f32[64,128]{1,0:T(8,128)}, /*index=5*/f32[64,128]{1,0:T(8,128)}) custom-call(f32[32,64,128]{2,1,0:T(8,128)} %get-tuple-element.12.refs_0_, f32[32,64,128]{2,1,0:T(8,128)} %get-tuple-element.13.refs_1_, ...), custom_call_target="tpu_custom_call" | custom-call | tf_op jit(solution)/shard_map/place/pallas_call | solution.py:568
